TPU v7x, 32 devices: a whole 2x2x4 slice. The times are simulated.
32 devices in a mesh: section: 2 (over core), fsdp: 2 (over x), ctx: 4 (over z), tp: 2 (over y).
Axes of the slice: x: 2, y: 2, z: 4, core: 2. Of those that a mesh axis runs over, the one named last changes fastest.
Arguments:
- boundary: bfloat16 [2, 2, 2, 1024, 2048], P('section', None, 'fsdp', 'ctx'), may hold values from -6 to 6
- segments: int32 [2, 2, 1024], P(None, 'fsdp'), may hold values from 0 to 2, as said below
- qkv_w: bfloat16 [2, 2048, 8, 384], P('section', ('fsdp', 'ctx'), 'tp'), may hold values from -0.125 to 0.125
- out_w: bfloat16 [2, 2048, 2048], P('section', 'tp', ('fsdp', 'ctx')), may hold values from -2 to 2
- gate_up_w: bfloat16 [2, 2048, 2, 8192], P('section', ('fsdp', 'ctx'), None, 'tp'), may hold values from -0.125 to 0.125
- down_w: bfloat16 [2, 8192, 2048], P('section', 'tp', ('fsdp', 'ctx')), may hold values from -0.0625 to 0.0625
- norm_gains: bfloat16 [2, 2, 2048], P('section', None, ('fsdp', 'ctx')), may hold values from 0.25 to 1.75
Outputs:
- boundary_out: float32 [2, 2, 2, 1024, 2048], P('section', None, 'fsdp', 'ctx')
- grad_qkv_w: float32 [2, 2048, 8, 384], P('section', ('fsdp', 'ctx'), 'tp')
- grad_out_w: float32 [2, 2048, 2048], P('section', 'tp', ('fsdp', 'ctx'))
- grad_gate_up_w: float32 [2, 2048, 2, 8192], P('section', ('fsdp', 'ctx'), None, 'tp')
- grad_down_w: float32 [2, 8192, 2048], P('section', 'tp', ('fsdp', 'ctx'))
- grad_norm_gains: float32 [2, 2048], P('section', ('fsdp', 'ctx'))
- grad_ffn_gains: float32 [2, 2048], P('section', ('fsdp', 'ctx'))
Inputs may be any that keep to these rules, and one draw needn't show every extreme that they name: `segments`: each sequence holds three documents numbered 0, 1, 2 in order; each has 204 tokens or more, and document 1 holds positions 511 and 512.
All inputs are finite; a program needn't handle non-finite values.
Results may differ from a plain program's by a relative error of at most 0.03.
Values may be sent and summed in bfloat16 or wider, within the bound.
No kernel may reach another device: no remote copies, remote signals or barrier semaphores. Data moves between devices by JAX's collectives and lax.ppermute only.
A program may use at most 512 MiB of HBM per device.

v0:
```python
from functools import partial

import jax
import jax.numpy as jnp
from jax import lax
from jax.sharding import PartitionSpec as P

H = 32
KV = 8
HD = 64


norm_eps = 1e-05
rope_base = 500000.0
masked_score = -1e30


def from_behind(value, axis, by):
    size = lax.axis_size(axis)
    pairs = [(i, i + by) for i in range(size) if 0 <= i + by < size]
    return lax.ppermute(value, axis, pairs)


def rotate(values, cosine, sine):
    half_dim = values.shape[-1] // 2
    turned = jnp.concatenate([-values[..., half_dim:], values[..., :half_dim]], axis=-1)
    return values * cosine + turned * sine


def rope_tables(positions):
    freq_index = jnp.arange(HD // 2, dtype=jnp.float32)
    inverse = rope_base ** (-2.0 * freq_index / HD)
    angles = positions.astype(jnp.float32)[:, None] * inverse[None, :]
    angles = jnp.concatenate([angles, angles], axis=-1)
    return (jnp.cos(angles), jnp.sin(angles))


def context_info(seg_full, ctx_index, rows):
    offsets = jnp.arange(rows, dtype=jnp.int32)
    query_pos = ctx_index * rows + offsets
    query_seg = lax.dynamic_slice_in_dim(seg_full, ctx_index * rows, rows)
    starts = jnp.sum((seg_full[None, :] < query_seg[:, None]).astype(jnp.int32), axis=1)
    cosine, sine = rope_tables(query_pos - starts)
    key_pos = jnp.arange(seg_full.shape[0], dtype=jnp.int32)
    return (cosine, sine, query_pos, query_seg, key_pos, seg_full)


def norm_rows(values, gain):
    scale_rows = lax.rsqrt(jnp.mean(values * values, axis=-1, keepdims=True) + norm_eps)
    return (values * scale_rows * gain, scale_rows)


def norm_back(values, scale_rows, gain, grad_normed):
    scaled = values * scale_rows
    grad_gain = jnp.sum(grad_normed * scaled, axis=0)
    grad_hat = grad_normed * gain
    grad_in = scale_rows * (grad_hat - scaled * jnp.mean(grad_hat * scaled, axis=-1, keepdims=True))
    return (grad_in, grad_gain)


def block_scores(query_block, pair, info):
    cosine, sine, query_pos, query_seg, key_pos, key_seg = info
    raw = jnp.einsum(
        "qkgd,tkd->kgqt", query_block, pair[0], preferred_element_type=jnp.float32
    ) * HD ** (-0.5)
    allowed = (key_pos[None, :] <= query_pos[:, None]) & (key_seg[None, :] == query_seg[:, None])
    return jnp.where(allowed[None, None], raw, masked_score)


def attend_forward(queries, pair, info):
    rows, kv_local, groups, head_dim = queries.shape
    block_rows = min(512, rows)
    block_count = rows // block_rows

    def one_block(item):
        query_block, block_index = item
        scores = block_scores(query_block, pair, info)
        top_score = jnp.max(scores, axis=-1, keepdims=True)
        weights = jnp.exp(scores - top_score)
        totals = jnp.sum(weights, axis=-1, keepdims=True)
        probs = (weights / totals).astype(jnp.bfloat16)
        output = jnp.einsum("kgqt,tkd->qkgd", probs, pair[1], preferred_element_type=jnp.float32)
        return (output, (top_score + jnp.log(totals))[..., 0])

    blocks = queries.reshape(block_count, block_rows, kv_local, groups, head_dim)
    outputs, log_sums = lax.map(one_block, (blocks, jnp.arange(block_count, dtype=jnp.int32)))
    return (outputs.reshape(rows, kv_local, groups, head_dim), log_sums)


def attend_backward(queries, pair, log_sums, grad_attended, info):
    rows, kv_local, groups, head_dim = queries.shape
    block_rows = min(512, rows)
    block_count = rows // block_rows
    scale = HD ** (-0.5)

    def step_block(carry, item):
        grad_keys, grad_values = carry
        query_block, grad_block, lse_block, block_index = item
        scores = block_scores(query_block, pair, info)
        probs = jnp.exp(scores - lse_block[..., None])
        grad_probs = jnp.einsum(
            "qkgd,tkd->kgqt", grad_block, pair[1], preferred_element_type=jnp.float32
        )
        delta = jnp.sum(probs * grad_probs, axis=-1, keepdims=True)
        grad_scores = (probs * (grad_probs - delta)).astype(jnp.bfloat16)
        grad_query = (
            jnp.einsum("kgqt,tkd->qkgd", grad_scores, pair[0], preferred_element_type=jnp.float32)
            * scale
        )
        grad_keys = (
            grad_keys
            + jnp.einsum(
                "kgqt,qkgd->tkd", grad_scores, query_block, preferred_element_type=jnp.float32
            )
            * scale
        )
        grad_values = grad_values + jnp.einsum(
            "kgqt,qkgd->tkd",
            probs.astype(jnp.bfloat16),
            grad_block,
            preferred_element_type=jnp.float32,
        )
        return ((grad_keys, grad_values), grad_query)

    start_grads = jnp.zeros(pair.shape[1:], jnp.float32)
    blocks = queries.reshape(block_count, block_rows, kv_local, groups, head_dim)
    grad_blocks = grad_attended.reshape(block_count, block_rows, kv_local, groups, head_dim)
    carry_out, grad_queries = lax.scan(
        step_block,
        (start_grads, start_grads),
        (blocks, grad_blocks, log_sums, jnp.arange(block_count, dtype=jnp.int32)),
    )
    return (
        grad_queries.reshape(rows, kv_local, groups, head_dim),
        jnp.stack([carry_out[0], carry_out[1]]),
    )


def feed_forward_in(middle, scale_two, gains, gate_up_full):
    ffn_in = (middle * scale_two * gains[1]).astype(jnp.bfloat16)
    gate_up = jnp.einsum("rd,dtf->rtf", ffn_in, gate_up_full, preferred_element_type=jnp.float32)
    hidden_low = (jax.nn.silu(gate_up[:, 0]) * gate_up[:, 1]).astype(jnp.bfloat16)
    return (ffn_in, gate_up, hidden_low)


def layer_forward(inputs, weights, info):
    qkv_full, out_full, gate_up_full, down_full, gains = weights
    cosine, sine = (info[0], info[1])
    rows = inputs.shape[0]
    full_rows = info[5].shape[0]
    kv_local = qkv_full.shape[1]
    groups = H // KV
    normed_one, scale_one = norm_rows(inputs, gains[0])
    attn_in = normed_one.astype(jnp.bfloat16)
    qkv = jnp.einsum("rd,dkc->rkc", attn_in, qkv_full, preferred_element_type=jnp.float32)
    queries = rotate(
        qkv[:, :, : groups * HD].reshape(rows, kv_local, groups, HD),
        cosine[:, None, None, :],
        sine[:, None, None, :],
    ).astype(jnp.bfloat16)
    keys_now = rotate(
        qkv[:, :, groups * HD : (groups + 1) * HD], cosine[:, None, :], sine[:, None, :]
    ).astype(jnp.bfloat16)
    values_now = qkv[:, :, (groups + 1) * HD :].astype(jnp.bfloat16)
    own_pair = jnp.stack([keys_now, values_now]).reshape(2, rows, kv_local * HD)
    pair = lax.all_gather(own_pair, "ctx", axis=1, tiled=True).reshape(2, full_rows, kv_local, HD)
    attended, log_sums = attend_forward(queries, pair, info)
    attended_low = attended.reshape(rows, kv_local * groups * HD).astype(jnp.bfloat16)
    middle = inputs + lax.psum(
        jnp.dot(attended_low, out_full, preferred_element_type=jnp.float32).astype(jnp.bfloat16),
        "tp",
    ).astype(jnp.float32)
    normed_two, scale_two = norm_rows(middle, gains[1])
    ffn_in, gate_up, hidden_low = feed_forward_in(middle, scale_two, gains, gate_up_full)
    result = middle + lax.psum(
        jnp.dot(hidden_low, down_full, preferred_element_type=jnp.float32).astype(jnp.bfloat16),
        "tp",
    ).astype(jnp.float32)
    ff_saved = (ffn_in, gate_up, hidden_low)
    return (
        result,
        (
            inputs,
            scale_one,
            attn_in,
            queries,
            pair,
            log_sums,
            attended_low,
            middle,
            scale_two,
            ff_saved,
        ),
    )


def layer_backward(saved, grad_out, weights, info):
    qkv_full, out_full, gate_up_full, down_full, gains = weights
    (
        inputs,
        scale_one,
        attn_in,
        queries,
        pair,
        log_sums,
        attended_low,
        middle,
        scale_two,
        ff_saved,
    ) = saved
    cosine, sine = (info[0], info[1])
    rows, kv_local, groups, head_dim = queries.shape
    full_rows = pair.shape[1]
    ffn_in, gate_up, hidden_low = ff_saved
    grad_low = grad_out.astype(jnp.bfloat16)
    grad_down = jnp.einsum("rf,rd->fd", hidden_low, grad_low, preferred_element_type=jnp.float32)
    grad_hidden = jnp.einsum("rd,fd->rf", grad_low, down_full, preferred_element_type=jnp.float32)
    gate = gate_up[:, 0]
    sigma = jax.nn.sigmoid(gate)
    grad_gate = grad_hidden * gate_up[:, 1] * sigma * (1.0 + gate * (1.0 - sigma))
    grad_up = grad_hidden * gate * sigma
    grad_pair_ff = jnp.stack([grad_gate, grad_up], axis=1).astype(jnp.bfloat16)
    grad_gate_up = jnp.einsum(
        "rd,rtf->dtf", ffn_in, grad_pair_ff, preferred_element_type=jnp.float32
    )
    grad_ffn_in = lax.psum(
        jnp.einsum(
            "rtf,dtf->rd", grad_pair_ff, gate_up_full, preferred_element_type=jnp.float32
        ).astype(jnp.bfloat16),
        "tp",
    ).astype(jnp.float32)
    grad_mid_norm, grad_gain_two = norm_back(middle, scale_two, gains[1], grad_ffn_in)
    grad_middle = grad_out + grad_mid_norm
    grad_attn_low = grad_middle.astype(jnp.bfloat16)
    grad_out_proj = jnp.einsum(
        "rh,rd->hd", attended_low, grad_attn_low, preferred_element_type=jnp.float32
    )
    grad_attended = jnp.einsum(
        "rd,hd->rh", grad_attn_low, out_full, preferred_element_type=jnp.float32
    ).astype(jnp.bfloat16)
    grad_queries, grad_pair = attend_backward(
        queries, pair, log_sums, grad_attended.reshape(rows, kv_local, groups, head_dim), info
    )
    returned = lax.psum_scatter(
        grad_pair.reshape(2, full_rows, kv_local * head_dim).astype(jnp.bfloat16),
        "ctx",
        scatter_dimension=1,
        tiled=True,
    ).astype(jnp.float32)
    own_grad = returned.reshape(2, rows, kv_local, head_dim)
    grad_q_raw = rotate(grad_queries, cosine[:, None, None, :], -sine[:, None, None, :]).reshape(
        rows, kv_local, groups * head_dim
    )
    grad_k_raw = rotate(own_grad[0], cosine[:, None, :], -sine[:, None, :])
    grad_qkv = jnp.concatenate([grad_q_raw, grad_k_raw, own_grad[1]], axis=-1).astype(jnp.bfloat16)
    grad_qkv_proj = jnp.einsum("rd,rkc->dkc", attn_in, grad_qkv, preferred_element_type=jnp.float32)
    grad_attn_in = lax.psum(
        jnp.einsum("rkc,dkc->rd", grad_qkv, qkv_full, preferred_element_type=jnp.float32).astype(
            jnp.bfloat16
        ),
        "tp",
    ).astype(jnp.float32)
    grad_in_norm, grad_gain_one = norm_back(inputs, scale_one, gains[0], grad_attn_in)
    grads = (
        grad_qkv_proj,
        grad_out_proj,
        grad_gate_up,
        grad_down,
        jnp.stack([grad_gain_one, grad_gain_two]),
    )
    return (grad_middle + grad_in_norm, grads)


def pick_section(is_first, first_value, second_value):
    return jnp.where(is_first, first_value, second_value)


def scale_by(factor, values):
    return values * factor


def local(boundary, segments, qkv_w, out_w, gate_up_w, down_w, norm_gains):
    micro_count = boundary.shape[1]
    rows = boundary.shape[3]
    width = boundary.shape[4]
    is_first = lax.axis_index("section") == 0
    ctx_index = lax.axis_index("ctx")
    local_ends = boundary[0, :, 0]
    seg_all = segments[:, 0]
    gathered = (
        lax.all_gather(qkv_w[0], ("fsdp", "ctx"), axis=0, tiled=True),
        lax.all_gather(out_w[0], ("fsdp", "ctx"), axis=1, tiled=True),
        lax.all_gather(gate_up_w[0], ("fsdp", "ctx"), axis=0, tiled=True),
        lax.all_gather(down_w[0], ("fsdp", "ctx"), axis=1, tiled=True),
        lax.all_gather(norm_gains[0], ("fsdp", "ctx"), axis=1, tiled=True),
    )
    weights = (gathered[0], gathered[1], gathered[2], gathered[3], gathered[4].astype(jnp.float32))
    chooser = partial(pick_section, is_first)
    received = jnp.zeros((rows, width), jnp.bfloat16)
    saved_list = []
    info_list = []
    outputs_list = []
    for tick_index in range(micro_count + 1):
        own_index = min(tick_index, micro_count - 1)
        prior_index = max(tick_index - 1, 0)
        seg_full = jnp.where(is_first, seg_all[own_index], seg_all[prior_index])
        info = context_info(seg_full, ctx_index, rows)
        inputs = jnp.where(is_first, local_ends[own_index], received).astype(jnp.float32)
        result, saved = layer_forward(inputs, weights, info)
        saved_list.append(saved)
        info_list.append(info)
        outputs_list.append(result)
        if tick_index < micro_count:
            received = from_behind(result.astype(jnp.bfloat16), "section", 1)
    grad_received = jnp.zeros((rows, width), jnp.float32)
    totals = None
    grad_list = []
    for tick_index in range(micro_count + 1):
        early = max(tick_index - 1, 0)
        late = min(tick_index + 1, micro_count)
        saved = jax.tree.map(chooser, saved_list[early], saved_list[late])
        info = jax.tree.map(chooser, info_list[early], info_list[late])
        own_grad = local_ends[min(tick_index, micro_count - 1)].astype(jnp.float32)
        grad_out = jnp.where(is_first, grad_received, own_grad)
        grad_inputs, grads = layer_backward(saved, grad_out, weights, info)
        valid = jnp.where(is_first, tick_index >= 1, tick_index < micro_count).astype(jnp.float32)
        grads = jax.tree.map(partial(scale_by, valid), grads)
        totals = grads if totals is None else jax.tree.map(jnp.add, totals, grads)
        grad_list.append(grad_inputs)
        if tick_index < micro_count:
            grad_received = from_behind(grad_inputs.astype(jnp.bfloat16), "section", -1).astype(
                grad_inputs.dtype
            )
    totals = (
        lax.psum_scatter(
            totals[0].astype(jnp.bfloat16), ("fsdp", "ctx"), scatter_dimension=0, tiled=True
        ).astype(jnp.float32),
        lax.psum_scatter(
            totals[1].astype(jnp.bfloat16), ("fsdp", "ctx"), scatter_dimension=1, tiled=True
        ).astype(jnp.float32),
        lax.psum_scatter(
            totals[2].astype(jnp.bfloat16), ("fsdp", "ctx"), scatter_dimension=0, tiled=True
        ).astype(jnp.float32),
        lax.psum_scatter(
            totals[3].astype(jnp.bfloat16), ("fsdp", "ctx"), scatter_dimension=1, tiled=True
        ).astype(jnp.float32),
        lax.psum_scatter(
            totals[4].astype(jnp.bfloat16), ("fsdp", "ctx"), scatter_dimension=1, tiled=True
        ).astype(jnp.float32),
    )
    ends_out = jnp.stack(
        [
            jnp.where(is_first, grad_list[micro_index + 1], outputs_list[micro_index + 1])
            for micro_index in range(micro_count)
        ]
    )
    return (
        ends_out[None, :, None],
        totals[0][None],
        totals[1][None],
        totals[2][None],
        totals[3][None],
        totals[4][0][None],
        totals[4][1][None],
    )


def solution(mesh):
    return jax.shard_map(
        local,
        mesh=mesh,
        in_specs=(
            P("section", None, "fsdp", "ctx", None),
            P(None, "fsdp", None),
            P("section", ("fsdp", "ctx"), "tp", None),
            P("section", "tp", ("fsdp", "ctx")),
            P("section", ("fsdp", "ctx"), None, "tp"),
            P("section", "tp", ("fsdp", "ctx")),
            P("section", None, ("fsdp", "ctx")),
        ),
        out_specs=(
            P("section", None, "fsdp", "ctx", None),
            P("section", ("fsdp", "ctx"), "tp", None),
            P("section", "tp", ("fsdp", "ctx")),
            P("section", ("fsdp", "ctx"), None, "tp"),
            P("section", "tp", ("fsdp", "ctx")),
            P("section", ("fsdp", "ctx")),
            P("section", ("fsdp", "ctx")),
        ),
        check_vma=False,
    )
```

profile of v0, /device:TPU:3, one launch (start us, length us, event | category | flops | bytes accessed | tf_op | source)
XLA Modules:
  0.0 3293.5 jit_solution(327216069190537793)
XLA Ops:
  16.3 16.7 all-gather
  33.4 76.3 %all-gather.19.cloned.1.call-done = bf16[1,2048,4,384]{3,1,2,0:T(8,128)(2,1)} async-done(((bf16[1,256,4,384]{3,1,2,0:T(8,128)(2,1)}), bf16[1,2048,4,384]{3,1,2,0:T(8,128)(2,1)}) %all-gather.19.cloned.1.call-update) | async-done | bytes 6291472 | tf_op jit(solution)/shard_map/all_gather | solution.py:291
  130.9 17.9 all-gather.13.cloned.1.call-done
  175.2 50.0 %all-gather.21.cloned.1.call-done = bf16[1,1024,2048]{2,1,0:T(8,128)(2,1)} async-done(((bf16[1,1024,256]{2,1,0:T(8,128)(2,1)}), bf16[1,1024,2048]{2,1,0:T(8,128)(2,1)}) %all-gather.21.cloned.1.call-update) | async-done | bytes 4194320 | tf_op jit(solution)/shard_map/all_gather | solution.py:292
  237.7 30.1 all-reduce.13.cloned.1.call-done
  271.8 635.8 %all-gather.23.cloned.1.call-done = bf16[1,2048,2,4096]{3,1,2,0:T(8,128)(2,1)} async-done(((bf16[1,256,2,4096]{3,1,2,0:T(8,128)(2,1)}), bf16[1,2048,2,4096]{3,1,2,0:T(8,128)(2,1)}) %all-gather.23.cloned.1.call-update) | async-done | bytes 33554448 | tf_op jit(solution)/shard_map/all_gather | solution.py:293
  907.6 15.1 fusion.10
  928.7 210.2 %all-gather.25.cloned.1.call-done = bf16[1,4096,2048]{2,1,0:T(8,128)(2,1)} async-done(((bf16[1,4096,256]{2,1,0:T(8,128)(2,1)}), bf16[1,4096,2048]{2,1,0:T(8,128)(2,1)}) %all-gather.25.cloned.1.call-update) | async-done | bytes 16777232 | tf_op jit(solution)/shard_map/all_gather | solution.py:294
  1138.9 11.9 fusion.129
  1150.8 38.1 %all-reduce.15.cloned.1.call-done = bf16[256,2048]{1,0:T(8,128)(2,1)} async-done(((bf16[256,2048]{1,0:T(8,128)(2,1)}), bf16[256,2048]{1,0:T(8,128)(2,1)}) %all-reduce.15.cloned.1.call-update) | async-done | bytes 1048592 | tf_op jit(solution)/shard_map/psum | solution.py:175
  1217.4 21.4 all-gather.15.cloned.1.call-done
  1268.1 39.1 %all-reduce.17.cloned.1.call-done = bf16[256,2048]{1,0:T(8,128)(2,1)} async-done(((bf16[256,2048]{1,0:T(8,128)(2,1)}), bf16[256,2048]{1,0:T(8,128)(2,1)}) %all-reduce.17.cloned.1.call-update) | async-done | bytes 1048592 | tf_op jit(solution)/shard_map/psum | solution.py:169
  1312.1 18.4 broadcast_select_fusion.2
  1334.6 12.6 fusion.220
  1356.5 16.7 fusion.126
  1373.5 64.8 %all-reduce.29.cloned.1.call-done = (bf16[256,2048]{1,0:T(8,128)(2,1)}, bf16[256,2048]{1,0:T(8,128)(2,1)}) async-done(((bf16[256,2048]{1,0:T(8,128)(2,1)}, bf16[256,2048]{1,0:T(8,128)(2,1)}), (bf16[256,2048]{1,0:T(8,128)(2,1)}, bf16[256,2048]{1,0:T(8,128)(2,1)})) %all-reduce.29.cloned.1.call-update) | async-done | bytes 2097168 | tf_op jit(solution)/shard_map/psum | solution.py:175
  1478.7 14.7 all-gather.17.cloned.1.call-done
  1523.7 14.2 fusion.22
  1547.5 10.5 fusion.24
  1582.5 15.6 reduce-scatter.11.cloned.1.call-done
  1606.5 62.0 %all-reduce.27.cloned.1.call-done = (bf16[256,2048]{1,0:T(8,128)(2,1)}, bf16[256,2048]{1,0:T(8,128)(2,1)}) async-done(((bf16[256,2048]{1,0:T(8,128)(2,1)}, bf16[256,2048]{1,0:T(8,128)(2,1)}), (bf16[256,2048]{1,0:T(8,128)(2,1)}, bf16[256,2048]{1,0:T(8,128)(2,1)})) %all-reduce.27.cloned.1.call-update) | async-done | bytes 2097168 | tf_op jit(solution)/shard_map/psum | solution.py:169
  1682.8 24.5 broadcast_select_fusion
  1707.3 13.0 fusion.221
  1720.3 16.7 fusion.123
  1739.7 39.4 %all-reduce.19.cloned.1.call-done = bf16[256,2048]{1,0:T(8,128)(2,1)} async-done(((bf16[256,2048]{1,0:T(8,128)(2,1)}), bf16[256,2048]{1,0:T(8,128)(2,1)}) %all-reduce.19.cloned.1.call-update) | async-done | bytes 1048592 | tf_op jit(solution)/shard_map/psum | solution.py:226
  1798.7 14.1 fusion.17
  1821.6 10.4 fusion.19
  1847.9 18.3 reduce-scatter.13.cloned.1.call-done
  1877.5 39.0 %all-reduce.21.cloned.1.call-done = bf16[256,2048]{1,0:T(8,128)(2,1)} async-done(((bf16[256,2048]{1,0:T(8,128)(2,1)}), bf16[256,2048]{1,0:T(8,128)(2,1)}) %all-reduce.21.cloned.1.call-update) | async-done | bytes 1048592 | tf_op jit(solution)/shard_map/psum | solution.py:257
  1931.8 12.9 fusion.222
  1944.8 16.7 fusion.120
  1967.8 33.4 %all-reduce.23.cloned.1.call-done = bf16[256,2048]{1,0:T(8,128)(2,1)} async-done(((bf16[256,2048]{1,0:T(8,128)(2,1)}), bf16[256,2048]{1,0:T(8,128)(2,1)}) %all-reduce.23.cloned.1.call-update) | async-done | bytes 1048592 | tf_op jit(solution)/shard_map/psum | solution.py:226
  2022.1 14.1 fusion.12
  2045.0 10.4 fusion.14
  2063.1 11.9 fusion.135
  2110.9 50.7 %all-reduce.25.cloned.1.call-done = (bf16[256,2048]{1,0:T(8,128)(2,1)}, bf16[256,2048]{1,0:T(8,128)(2,1)}) async-done(((bf16[256,2048]{1,0:T(8,128)(2,1)}, bf16[256,2048]{1,0:T(8,128)(2,1)}), (bf16[256,2048]{1,0:T(8,128)(2,1)}, bf16[256,2048]{1,0:T(8,128)(2,1)})) %all-reduce.25.cloned.1.call-update) | async-done | bytes 2097168 | tf_op jit(solution)/shard_map/psum | solution.py:257
  2166.4 10.2 add_convert_fusion.3
  2192.7 13.1 add_convert_fusion.2
  2206.1 17.7 fusion.207
  2223.8 18.0 fusion.210
  2241.7 30.3 add_convert_fusion.1
  2273.6 25.8 fusion.119
  2299.4 26.1 fusion.118
  2325.5 56.6 %add_convert_fusion = bf16[2048,2,4096]{2,0,1:T(8,128)(2,1)} fusion(f32[2048,2,4096]{2,0,1:T(8,128)} %fusion.118, f32[2048,2,4096]{2,0,1:T(8,128)} %fusion.119, f32[]{:T(128)S(6)} %convert_element_type.420, f32[]{:T(128)S(6)} %convert_element_type.419, bf16[256,1,4096]{2,0,1:T(8,128)(2,1)} %get-tuple-element.258, ...), kind=kOutput, calls=%fused_computation | convolution fusion | flops 8682733568 | bytes 174063632 | tf_op jit(solution)/shard_map/rd,rtf->dtf/dot_general | solution.py:223
  2393.7 47.3 %reduce-scatter.17.cloned.1.call-done = bf16[256,4,384]{2,0,1:T(8,128)(2,1)} async-done(((bf16[2048,4,384]{2,0,1:T(8,128)(2,1)}), bf16[256,4,384]{2,0,1:T(8,128)(2,1)}) %reduce-scatter.17.cloned.1.call-update) | async-done | bytes 786448 | tf_op jit(solution)/shard_map/reduce_scatter | solution.py:335
  2444.4 282.4 %reduce-scatter.23.cloned.1.call-done = bf16[4096,256]{1,0:T(8,128)(2,1)} async-done(((bf16[4096,2048]{1,0:T(8,128)(2,1)}), bf16[4096,256]{1,0:T(8,128)(2,1)}) %reduce-scatter.23.cloned.1.call-update) | async-done | bytes 2097168 | tf_op jit(solution)/shard_map/reduce_scatter | solution.py:344
  2730.8 542.5 %reduce-scatter.21.cloned.1.call-done = bf16[256,2,4096]{2,0,1:T(8,128)(2,1)} async-done(((bf16[2048,2,4096]{2,0,1:T(8,128)(2,1)}), bf16[256,2,4096]{2,0,1:T(8,128)(2,1)}) %reduce-scatter.21.cloned.1.call-update) | async-done | bytes 4194320 | tf_op jit(solution)/shard_map/reduce_scatter | solution.py:341
  3276.5 9.8 copy.252
  (542 shorter events, 479.5 us)
Async XLA Ops:
  7.2 102.5 %all-gather.19.cloned.1.call-start = ((), (), s32[]{:S(2)}) async-start(), calls=%async_computation.24 | async-start | bytes 7077888 | tf_op jit(solution)/shard_map/all_gather | solution.py:291
  9.5 139.3 %all-gather.13.cloned.1.call-start = ((), (), s32[]{:S(2)}) async-start(), calls=%async_computation.8 | async-start | bytes 1310720 | tf_op jit(solution)/shard_map/all_gather | solution.py:166
  12.3 102.0 %copy-start.79 = (f32[256,32]{0,1:T(8,128)}, f32[256,32]{0,1:T(8,128)S(1)}, u32[]{:S(2)}) copy-start(f32[256,32]{0,1:T(8,128)S(1)} %get-tuple-element.357) | copy-start | bytes 98308
  33.3 81.0 %copy-start.125 = (f32[256]{0:T(256)}, f32[256]{0:T(256)S(1)}, u32[]{:S(2)}) copy-start(f32[256]{0:T(256)S(1)} %fusion.202) | copy-start | bytes 3076
  33.4 81.0 %copy-start.120 = (f32[256]{0:T(256)}, f32[256]{0:T(256)S(1)}, u32[]{:S(2)}) copy-start(f32[256]{0:T(256)S(1)} %add_rsqrt_fusion.5) | copy-start | bytes 3076
  33.4 2159.3 %copy-start.70 = (f32[1,1,2048]{2,1,0:T(1,128)}, f32[1,1,2048]{2,1,0:T(1,128)S(1)}, u32[]{:S(2)}) copy-start(f32[1,1,2048]{2,1,0:T(1,128)S(1)} %get-tuple-element.337) | copy-start | bytes 24580
  119.7 105.5 %all-gather.21.cloned.1.call-start = ((), (), s32[]{:S(2)}) async-start(), calls=%async_computation.25 | async-start | bytes 4718592 | tf_op jit(solution)/shard_map/all_gather | solution.py:292
  120.4 147.4 %all-reduce.13.cloned.1.call-start = ((), (), s32[]{:S(2)}) async-start(), calls=%async_computation.9 | async-start | bytes 2097152 | tf_op jit(solution)/shard_map/psum | solution.py:169
  175.1 61.7 %copy-start.37 = (bf16[4,64,4,256]{3,1,2,0:T(8,128)(2,1)}, bf16[4,64,4,256]{3,1,2,0:T(8,128)(2,1)S(1)}, u32[]{:S(2)}) copy-start(bf16[4,64,4,256]{3,1,2,0:T(8,128)(2,1)S(1)} %fusion.261) | copy-start | bytes 1572868
  229.7 677.9 %all-gather.23.cloned.1.call-start = ((), (), s32[]{:S(2)}) async-start(), calls=%async_computation.26 | async-start | bytes 37748736 | tf_op jit(solution)/shard_map/all_gather | solution.py:293
  236.8 902.0 %all-gather.25.cloned.1.call-start = ((), (), s32[]{:S(2)}) async-start(), calls=%async_computation.27 | async-start | bytes 18874368 | tf_op jit(solution)/shard_map/all_gather | solution.py:294
  237.4 951.5 %all-reduce.15.cloned.1.call-start = ((), (), s32[]{:S(2)}) async-start(), calls=%async_computation.10 | async-start | bytes 2097152 | tf_op jit(solution)/shard_map/psum | solution.py:175
  271.8 650.9 %copy-start.14 = (bf16[256,2048]{1,0:T(8,128)(2,1)}, bf16[256,2048]{1,0:T(8,128)(2,1)S(1)}, u32[]{:S(2)}) copy-start(bf16[256,2048]{1,0:T(8,128)(2,1)S(1)} %multiply_convert_fusion.9) | copy-start | bytes 3145732
  928.7 260.3 %copy-start.3 = (bf16[1,2,1,256,2048]{4,3,2,1,0:T(8,128)(2,1)S(1)}, bf16[1,2,1,256,2048]{4,3,2,1,0:T(8,128)(2,1)}, u32[]{:S(2)}) copy-start(bf16[1,2,1,256,2048]{4,3,2,1,0:T(8,128)(2,1)} %param.7) | copy-start | bytes 6291460
  1150.7 88.1 %all-gather.15.cloned.1.call-start = ((), (), s32[]{:S(2)}) async-start(), calls=%async_computation.11 | async-start | bytes 1310720 | tf_op jit(solution)/shard_map/all_gather | solution.py:166
  1192.0 4.9 collective-permute-start
  1209.8 97.4 %all-reduce.17.cloned.1.call-start = ((), (), s32[]{:S(2)}) async-start(), calls=%async_computation.12 | async-start | bytes 2097152 | tf_op jit(solution)/shard_map/psum | solution.py:169
  1217.4 340.6 %copy-start.18 = (bf16[256,4,4,64]{0,3,2,1:T(8,128)(2,1)}, bf16[256,4,4,64]{0,3,2,1:T(8,128)(2,1)S(1)}, u32[]{:S(2)}) copy-start(bf16[256,4,4,64]{0,3,2,1:T(8,128)(2,1)S(1)} %fusion.267) | copy-start | bytes 1572868
  1267.9 170.4 %all-reduce.29.cloned.1.call-start = ((), (), s32[]{:S(2)}) async-start(), calls=%async_computation.31 | async-start | bytes 4194304 | tf_op jit(solution)/shard_map/psum | solution.py:175
  1309.2 137.4 %copy-start.123 = (f32[256]{0:T(256)}, f32[256]{0:T(256)S(1)}, u32[]{:S(2)}) copy-start(f32[256]{0:T(256)S(1)} %get-tuple-element.354) | copy-start | bytes 3076
  1373.2 69.8 %copy-start.75 = (f32[256,64]{0,1:T(8,128)S(1)}, f32[256,64]{0,1:T(8,128)}, u32[]{:S(2)}) copy-start(f32[256,64]{0,1:T(8,128)} %get-tuple-element.326) | copy-start | bytes 196612
  1373.2 69.9 %copy-start.76 = (f32[256,64]{0,1:T(8,128)S(1)}, f32[256,64]{0,1:T(8,128)}, u32[]{:S(2)}) copy-start(f32[256,64]{0,1:T(8,128)} %get-tuple-element.327) | copy-start | bytes 196612
  1373.2 70.0 %copy-start.84 = (f32[256,64]{0,1:T(8,128)S(1)}, f32[256,64]{0,1:T(8,128)}, u32[]{:S(2)}) copy-start(f32[256,64]{0,1:T(8,128)} %get-tuple-element.320) | copy-start | bytes 196612
  1373.2 70.1 %copy-start.73 = (f32[256,64]{0,1:T(8,128)S(1)}, f32[256,64]{0,1:T(8,128)}, u32[]{:S(2)}) copy-start(f32[256,64]{0,1:T(8,128)} %get-tuple-element.318) | copy-start | bytes 196612
  1373.2 120.2 %all-gather.17.cloned.1.call-start = ((), (), s32[]{:S(2)}) async-start(), calls=%async_computation.14 | async-start | bytes 1310720 | tf_op jit(solution)/shard_map/all_gather | solution.py:166
  1441.7 4.9 collective-permute-start.2
  1464.4 133.8 %reduce-scatter.11.cloned.1.call-start = ((), (), s32[]{:S(2)}) async-start(), calls=%async_computation.13 | async-start | bytes 1310720 | tf_op jit(solution)/shard_map/reduce_scatter | solution.py:244
  1571.9 96.6 %all-reduce.27.cloned.1.call-start = ((), (), s32[]{:S(2)}) async-start(), calls=%async_computation.30 | async-start | bytes 4194304 | tf_op jit(solution)/shard_map/psum | solution.py:169
  1606.4 64.2 %copy-start.108 = (f32[256]{0:T(256)S(1)}, f32[256]{0:T(256)}, u32[]{:S(2)}) copy-start(f32[256]{0:T(256)} %copy-done.106) | copy-start | bytes 3076
  1606.4 64.2 %copy-start.128 = (f32[256]{0:T(256)S(1)}, f32[256]{0:T(256)}, u32[]{:S(2)}) copy-start(f32[256]{0:T(256)} %copy-done.127) | copy-start | bytes 3076
  1606.4 172.7 %all-reduce.19.cloned.1.call-start = ((), (), s32[]{:S(2)}) async-start(), calls=%async_computation.15 | async-start | bytes 2097152 | tf_op jit(solution)/shard_map/psum | solution.py:226
  1679.3 28.0 collective-permute-start.1
  1737.0 129.3 %reduce-scatter.13.cloned.1.call-start = ((), (), s32[]{:S(2)}) async-start(), calls=%async_computation.16 | async-start | bytes 1310720 | tf_op jit(solution)/shard_map/reduce_scatter | solution.py:244
  1839.1 77.4 %all-reduce.21.cloned.1.call-start = ((), (), s32[]{:S(2)}) async-start(), calls=%async_computation.17 | async-start | bytes 2097152 | tf_op jit(solution)/shard_map/psum | solution.py:257
  1877.5 123.7 %all-reduce.23.cloned.1.call-start = ((), (), s32[]{:S(2)}) async-start(), calls=%async_computation.18 | async-start | bytes 2097152 | tf_op jit(solution)/shard_map/psum | solution.py:226
  1925.2 6.7 collective-permute-start.3
  1961.5 128.2 %reduce-scatter.15.cloned.1.call-start = ((), (), s32[]{:S(2)}) async-start(), calls=%async_computation.19 | async-start | bytes 1310720 | tf_op jit(solution)/shard_map/reduce_scatter | solution.py:244
  2062.6 99.1 %all-reduce.25.cloned.1.call-start = ((), (), s32[]{:S(2)}) async-start(), calls=%async_computation.29 | async-start | bytes 4194304 | tf_op jit(solution)/shard_map/psum | solution.py:257
  2099.6 290.5 %reduce-scatter.25.cloned.1.call-start = ((), (), s32[]{:S(2)}) async-start(), calls=%async_computation.28 | async-start | bytes 589824
  2106.3 55.3 %copy-start.118 = (f32[256]{0:T(256)S(1)}, f32[256]{0:T(256)}, u32[]{:S(2)}) copy-start(f32[256]{0:T(256)} %get-tuple-element.340) | copy-start | bytes 3076
  2106.3 58.7 %copy-start.102 = (f32[2048]{0:T(1024)S(1)}, f32[2048]{0:T(1024)}, u32[]{:S(2)}) copy-start(f32[2048]{0:T(1024)} %get-tuple-element.268) | copy-start | bytes 24580
  2106.4 58.7 %copy-start.103 = (f32[2048]{0:T(1024)S(1)}, f32[2048]{0:T(1024)}, u32[]{:S(2)}) copy-start(f32[2048]{0:T(1024)} %get-tuple-element.188) | copy-start | bytes 24580
  2106.4 58.7 %copy-start.104 = (f32[2048]{0:T(1024)S(1)}, f32[2048]{0:T(1024)}, u32[]{:S(2)}) copy-start(f32[2048]{0:T(1024)} %get-tuple-element.208) | copy-start | bytes 24580
  2110.9 55.5 %copy-start.50 = (bf16[4,64,4,256]{3,1,2,0:T(8,128)(2,1)S(1)}, bf16[4,64,4,256]{3,1,2,0:T(8,128)(2,1)}, u32[]{:S(2)}) copy-start(bf16[4,64,4,256]{3,1,2,0:T(8,128)(2,1)} %copy-done.49) | copy-start | bytes 1572868
  2166.2 225.4 %reduce-scatter.19.cloned.1.call-start = ((), (), s32[]{:S(2)}) async-start(), calls=%async_computation.21 | async-start | bytes 4718592 | tf_op jit(solution)/shard_map/reduce_scatter | solution.py:338
  2176.7 264.3 %reduce-scatter.17.cloned.1.call-start = ((), (), s32[]{:S(2)}) async-start(), calls=%async_computation.20 | async-start | bytes 7077888 | tf_op jit(solution)/shard_map/reduce_scatter | solution.py:335
  2205.8 521.0 %reduce-scatter.23.cloned.1.call-start = ((), (), s32[]{:S(2)}) async-start(), calls=%async_computation.23 | async-start | bytes 18874368 | tf_op jit(solution)/shard_map/reduce_scatter | solution.py:344
  2272.1 1001.2 %reduce-scatter.21.cloned.1.call-start = ((), (), s32[]{:S(2)}) async-start(), calls=%async_computation.22 | async-start | bytes 37748736 | tf_op jit(solution)/shard_map/reduce_scatter | solution.py:341
  (127 other events, 1126.2 us)
Sparse Core Ops, SparseCore 0:
  10.7 98.9 all-gather.18
  119.8 28.9 all-gather.12
  150.8 74.3 all-gather.20
  229.8 38.0 all-reduce.12
  269.9 637.6 all-gather.22
  909.6 229.1 all-gather.24
  1150.9 38.0 all-reduce.14
  1209.9 28.8 all-gather.14
  1268.0 39.1 all-reduce.16
  1373.3 64.8 all-reduce.28
  1464.5 28.8 all-gather.16
  1572.0 26.0 reduce-scatter.10
  1606.6 61.9 all-reduce.26
  1737.1 41.9 all-reduce.18
  1839.2 26.9 reduce-scatter.12
  1877.6 38.8 all-reduce.20
  1961.6 39.5 all-reduce.22
  2062.7 26.9 reduce-scatter.14
  2099.7 61.9 all-reduce.24
  2166.3 59.8 reduce-scatter.24
  2230.8 89.6 reduce-scatter.18
  2324.1 116.8 reduce-scatter.16
  2444.8 282.0 reduce-scatter.22
  2730.9 542.3 reduce-scatter.20
where the time goes:
time: 3300 us; the launch traced here: 3290 us
  waiting for transfers between devices  2340 us (71%)
  matrix products  623 us (19%)
  other arithmetic  191 us (6%)
  local copies, waits for them, and re-layouts  88.6 us (3%)
    all_gather x1, waiting for transfers between devices, local(): lax.all_gather(gate_up_w[0], ('fsdp', 'ctx'), axis=0, tiled=True)  636 us
    reduce_scatter x1, waiting for transfers between devices, local(): lax.psum_scatter(totals[2].astype(jnp.bfloat16), ('fsdp', 'ctx'), scatter...  543 us
    reduce_scatter x1, waiting for transfers between devices, local(): lax.psum_scatter(totals[3].astype(jnp.bfloat16), ('fsdp', 'ctx'), scatter...  282 us
    all_gather x1, waiting for transfers between devices, local(): lax.all_gather(down_w[0], ('fsdp', 'ctx'), axis=1, tiled=True)  210 us
    psum x3, waiting for transfers between devices, layer_forward(): lax.psum(jnp.dot(attended_low, out_full, preferred_element_type=jnp.float...  131 us
    dot_general x3, matrix products, layer_backward(): jnp.einsum('rd,rtf->dtf', ffn_in, grad_pair_ff, preferred_element_type=jn...  109 us
    psum x2, waiting for transfers between devices, layer_forward(): lax.psum(jnp.dot(hidden_low, down_full, preferred_element_type=jnp.float3...  103 us
    psum x2, waiting for transfers between devices, layer_backward(): lax.psum(jnp.einsum('rkc,dkc->rd', grad_qkv, qkv_full, preferred_element_...  89.7 us
  transfers between devices with their start and end apart: 28, of which 24 were waited for; matrix products, arithmetic and copies ran while one was open for 12% of the time, Pallas kernels for 0%

commit v1 on v0

--- a/solution.py
+++ b/solution.py
@@ -3,16 +3,21 @@
 import jax
 import jax.numpy as jnp
 from jax import lax
+from jax.experimental import pallas as pl
+from jax.experimental.pallas import tpu as pltpu
 from jax.sharding import PartitionSpec as P
 
 H = 32
 KV = 8
 HD = 64
-
+GROUPS = H // KV
 
 norm_eps = 1e-05
 rope_base = 500000.0
 masked_score = -1e30
+
+f32 = jnp.float32
+bf16 = jnp.bfloat16
 
 
 def from_behind(value, axis, by):
@@ -50,7 +55,7 @@
     return (values * scale_rows * gain, scale_rows)
 
 
-def norm_back(values, scale_rows, gain, grad_normed):
+def plain_norm_back(values, scale_rows, gain, grad_normed):
     scaled = values * scale_rows
     grad_gain = jnp.sum(grad_normed * scaled, axis=0)
     grad_hat = grad_normed * gain
@@ -67,7 +72,7 @@
     return jnp.where(allowed[None, None], raw, masked_score)
 
 
-def attend_forward(queries, pair, info):
+def plain_attend_forward(queries, pair, info):
     rows, kv_local, groups, head_dim = queries.shape
     block_rows = min(512, rows)
     block_count = rows // block_rows
@@ -87,7 +92,7 @@
     return (outputs.reshape(rows, kv_local, groups, head_dim), log_sums)
 
 
-def attend_backward(queries, pair, log_sums, grad_attended, info):
+def plain_attend_backward(queries, pair, log_sums, grad_attended, info):
     rows, kv_local, groups, head_dim = queries.shape
     block_rows = min(512, rows)
     block_count = rows // block_rows
@@ -164,7 +169,7 @@
     values_now = qkv[:, :, (groups + 1) * HD :].astype(jnp.bfloat16)
     own_pair = jnp.stack([keys_now, values_now]).reshape(2, rows, kv_local * HD)
     pair = lax.all_gather(own_pair, "ctx", axis=1, tiled=True).reshape(2, full_rows, kv_local, HD)
-    attended, log_sums = attend_forward(queries, pair, info)
+    attended, log_sums = plain_attend_forward(queries, pair, info)
     attended_low = attended.reshape(rows, kv_local * groups * HD).astype(jnp.bfloat16)
     middle = inputs + lax.psum(
         jnp.dot(attended_low, out_full, preferred_element_type=jnp.float32).astype(jnp.bfloat16),
@@ -229,7 +234,7 @@
         ).astype(jnp.bfloat16),
         "tp",
     ).astype(jnp.float32)
-    grad_mid_norm, grad_gain_two = norm_back(middle, scale_two, gains[1], grad_ffn_in)
+    grad_mid_norm, grad_gain_two = plain_norm_back(middle, scale_two, gains[1], grad_ffn_in)
     grad_middle = grad_out + grad_mid_norm
     grad_attn_low = grad_middle.astype(jnp.bfloat16)
     grad_out_proj = jnp.einsum(
@@ -238,7 +243,7 @@
     grad_attended = jnp.einsum(
         "rd,hd->rh", grad_attn_low, out_full, preferred_element_type=jnp.float32
     ).astype(jnp.bfloat16)
-    grad_queries, grad_pair = attend_backward(
+    grad_queries, grad_pair = plain_attend_backward(
         queries, pair, log_sums, grad_attended.reshape(rows, kv_local, groups, head_dim), info
     )
     returned = lax.psum_scatter(
@@ -260,7 +265,7 @@
         ),
         "tp",
     ).astype(jnp.float32)
-    grad_in_norm, grad_gain_one = norm_back(inputs, scale_one, gains[0], grad_attn_in)
+    grad_in_norm, grad_gain_one = plain_norm_back(inputs, scale_one, gains[0], grad_attn_in)
     grads = (
         grad_qkv_proj,
         grad_out_proj,
@@ -365,9 +370,776 @@
     )
 
 
+def swap_core(value):
+    return lax.ppermute(value, "section", [(0, 1), (1, 0)])
+
+
+def swap_tp(value):
+    return lax.ppermute(value, "tp", [(0, 1), (1, 0)])
+
+
+def swap_fsdp(value):
+    return lax.ppermute(value, "fsdp", [(0, 1), (1, 0)])
+
+
+def swap_ctx(value, m):
+    return lax.ppermute(value, "ctx", [(i ^ m, i) for i in range(lax.axis_size("ctx"))])
+
+
+def pick(bit, first, second):
+    return jnp.where(bit == 0, first, second)
+
+
+def ring(value):
+    size = lax.axis_size("ctx")
+    return lax.ppermute(value, "ctx", [(i, (i + 1) % size) for i in range(size)])
+
+
+def ring_back(value):
+    size = lax.axis_size("ctx")
+    return lax.ppermute(value, "ctx", [((i + 1) % size, i) for i in range(size)])
+
+
+class Flow:
+    def __init__(self):
+        self.values, self.next, self.last, self.first = {}, {}, None, None
+
+    def put(self, name, n, value):
+        self.values[name, n] = value
+
+    def get(self, name, n):
+        return self.values[name, n]
+
+    def send(self, name, n, move, value, made=False):
+        if self.last is not None:
+            if made:
+                self.next[self.last] = value
+                self.first = value if self.first is None else self.first
+            value, _ = lax.optimization_barrier((value, self.values[self.last]))
+        self.put(name, n, move(value))
+        self.last = (name, n)
+
+    def point(self, name, n, value):
+        names = DUE.get((name, n), ())
+        if names or isinstance(value, tuple):
+            ready = [self.next[k] for k in names if k in self.next]
+            value, *got = lax.optimization_barrier((value, *[self.values[k] for k in names], *ready))
+            self.values.update(zip(names, got))
+        return value
+
+
+def dot(a, b, dims):
+    return lax.dot_general(a, b, (dims, ((), ())), preferred_element_type=f32)
+
+
+NN = ((1,), (0,))
+NT = ((1,), (1,))
+TN = ((0,), (0,))
+VMEM = pl.BlockSpec(memory_space=pltpu.VMEM)
+SMEM = pl.BlockSpec(memory_space=pltpu.SMEM)
+COST_SCALE = 0.1
+VMEM_MIB = 28
+A_MID, A_IN, ATT, S_MID, S_HALF, MIDDLE, B_MID, B_IN, HIDDEN, R_MID, R_HALF, RESULT = range(12)
+G_MID, G_IN, D_HID, C_MID, C_HALF, D_MID, M_MID, M_IN, D_OUT, D_KEYS, D_QKV, E_MID, E_HALF, D_IN = range(12, 26)
+A0, F0, F1, F2, F3, E0, E1, E2, E3, H1, H2, H3, HX, ATTN_SUM = range(14)
+G1, G2, G3, GX, FFN_SUM, L1, L2, L3, LX, LOW_SUM, ENDS = range(17, 28)
+DUE = {
+    (HIDDEN, 0): ((ENDS, 1),),
+    (RESULT, 0): ((F1, 1),),
+    (S_MID, 1): ((F2, 1),),
+    (C_MID, 1): ((G1, 1),),
+    (M_MID, 1): ((L1, 1),),
+    (D_OUT, 1): ((G2, 1),),
+    (D_QKV, 1): ((L2, 1),),
+    (D_IN, 1): ((G3, 1),),
+    (D_HID, 0): ((L3, 1), (GX, 1)),
+    (D_MID, 0): ((H3, 1), (LX, 1)),
+    (D_OUT, 0): ((G1, 0),),
+    (D_KEYS, 0): ((L1, 0), (HX, 1)),
+    (D_IN, 0): ((H3, 0),),
+}
+
+
+def call(kernel, outs, ins, flops, name, **kw):
+    args = dict(in_specs=[SMEM if v.dtype == jnp.int32 and v.ndim == 1 else VMEM for v in ins], out_specs=[VMEM] * len(outs))
+    args.update(kw)
+    return pl.pallas_call(
+        kernel,
+        out_shape=[jax.ShapeDtypeStruct(s, d) for s, d in outs],
+        cost_estimate=pl.CostEstimate(flops=int(flops * COST_SCALE), bytes_accessed=1024, transcendentals=0),
+        compiler_params=pltpu.CompilerParams(vmem_limit_bytes=VMEM_MIB * 2**20),
+        name=name.__name__,
+        **args,
+    )(*ins)
+
+
+def views(refs):
+    return [r if k is None else r.at[k] for r in refs for k in ([None] if len(r.shape) == 2 else range(r.shape[0]))]
+
+
+def block_spec(array, width, where):
+    if array.ndim == 2:
+        return pl.BlockSpec((array.shape[0], width), lambda t: (0, where(t)))
+    return pl.BlockSpec(array.shape[:2] + (width,), lambda t: (0, 0, where(t)))
+
+
+def cols(index, width):
+    return pl.ds(pl.multiple_of(index * width, width), width)
+
+
+def rope(x, cosine, sin_up, sin_down):
+    return x * cosine + pltpu.roll(x, 96, 1) * sin_up + pltpu.roll(x, 32, 1) * sin_down
+
+
+def kv_tables(cosine, sin_up, sin_down):
+    is_key = lax.broadcasted_iota(jnp.int32, cosine.shape, 1) < HD
+    return (jnp.where(is_key, cosine, 1.0), jnp.where(is_key, sin_up, 0.0), jnp.where(is_key, sin_down, 0.0))
+
+
+def qkv_forward(order, spots, near, far, tables, blocks):
+    rows, width = near.shape
+    nb = order.shape[0]
+    bw = width // nb
+    qw = GROUPS * HD
+    part_rows = rows // 4
+
+    def kernel(order, spots, near, far, cosine, sin_up, sin_down, *refs):
+        w, (q_ref, kv_ref, wide) = views(refs[:-3]), refs[-3:]
+        for k in range(nb):
+            wide[cols(order[k], bw), :] = w[k][:, : qw + 2 * HD]
+        for part, a in enumerate((near, far)):
+            for half in range(2):
+                acc = dot(a[half * 2 * part_rows : (half + 1) * 2 * part_rows, :], wide[...], NN)
+                for t in range(2):
+                    there = cols(spots[4 * part + 2 * half + t], part_rows)
+                    v = acc[t * part_rows : (t + 1) * part_rows, :]
+                    tabs = (cosine[there, :], sin_up[there, :], sin_down[there, :])
+                    for j in range(qw // 128):
+                        here = slice(128 * j, 128 * (j + 1))
+                        q_ref[there, here] = (rope(v[:, here], *tabs) * HD**-0.5).astype(bf16)
+                    kv_ref[there, :] = rope(v[:, qw:], *kv_tables(*tabs)).astype(bf16)
+
+    return call(
+        kernel,
+        [((2 * rows, qw), bf16), ((2 * rows, 2 * HD), bf16)],
+        [order, spots, near, far, *tables, *blocks],
+        2 * 2 * rows * width * (qw + 2 * HD),
+        qkv_forward,
+        scratch_shapes=[pltpu.VMEM((width, qw + 2 * HD), bf16)],
+    )
+
+
+def keep_mask(start, first, rows, keys):
+    q_pos = first + lax.broadcasted_iota(jnp.int32, (rows, keys), 0)
+    k_pos = lax.broadcasted_iota(jnp.int32, (rows, keys), 1)
+    return jnp.where((k_pos <= q_pos) & (k_pos >= start), 0.0, masked_score)
+
+
+def attend_forward(spots, q, kv, start):
+    total, qw = q.shape
+    rows = total // 4
+    part_rows = total // 8
+
+    def kernel(spots, q_ref, kv_ref, start_ref, att_ref, lse_ref):
+        for i in range(4):
+            here = slice(i * rows, (i + 1) * rows)
+            keys = (i + 1) * rows
+            k, v = kv_ref[:keys, :HD], kv_ref[:keys, HD:]
+            bias = keep_mask(start_ref[here, :], i * rows, rows, keys)
+            for g in range(GROUPS):
+                head = slice(g * HD, (g + 1) * HD)
+                s = dot(q_ref[here, head], k, NT) + bias
+                top = jnp.max(s, axis=1, keepdims=True)
+                p = jnp.exp(s - top)
+                norm = jnp.sum(p, axis=1, keepdims=True)
+                o = (dot(p.astype(bf16), v, NN) / norm).astype(bf16)
+                for t in range(2):
+                    att_ref[cols(spots[2 * i + t], part_rows), head] = o[t * part_rows : (t + 1) * part_rows, :]
+                lse_ref[here, g : g + 1] = top + jnp.log(norm)
+
+    return call(
+        kernel,
+        [((total, qw), bf16), ((total, GROUPS), f32)],
+        [spots, q, kv, start],
+        2 * 2 * total * total * qw,
+        attend_forward,
+    )
+
+
+def attend_backward(spots, q, kv, lse, grad, start, tables):
+    total, qw = q.shape
+    rows = total // 4
+    part_rows = total // 8
+
+    def kernel(spots, q_ref, kv_ref, lse_ref, g_ref, start_ref, cosine, sin_up, sin_down, out, dq, dkv):
+        dkv[...] = jnp.zeros_like(dkv)
+        for i in range(4):
+            here = slice(i * rows, (i + 1) * rows)
+            keys = (i + 1) * rows
+            k, v = kv_ref[:keys, :HD], kv_ref[:keys, HD:]
+            bias = keep_mask(start_ref[here, :], i * rows, rows, keys)
+            grads = jnp.concatenate([g_ref[cols(spots[2 * i + t], part_rows), :] for t in range(2)], axis=0)
+            for g in range(GROUPS):
+                head = slice(g * HD, (g + 1) * HD)
+                qh, gh = q_ref[here, head], grads[:, head]
+                p = jnp.exp(dot(qh, k, NT) + bias - lse_ref[here, g : g + 1])
+                dp = dot(gh, v, NT)
+                delta = jnp.sum(p * dp, axis=1, keepdims=True)
+                ds = (p * (dp - delta)).astype(bf16)
+                dq[here, head] = dot(ds, k, NN) * HD**-0.5
+                dkv[:keys, :HD] += dot(ds, qh, TN)
+                dkv[:keys, HD:] += dot(p.astype(bf16), gh, TN)
+        for j in range(8):
+            here, there = slice(j * part_rows, (j + 1) * part_rows), cols(spots[j], part_rows)
+            tabs = (cosine[here, :], -sin_up[here, :], -sin_down[here, :])
+            for b in range(qw // 128):
+                out[there, 128 * b : 128 * (b + 1)] = rope(dq[here, 128 * b : 128 * (b + 1)], *tabs).astype(bf16)
+            out[there, qw:] = rope(dkv[here, :], *kv_tables(*tabs)).astype(bf16)
+
+    return call(
+        kernel,
+        [((total, qw + 2 * HD), bf16)],
+        [spots, q, kv, lse, grad, start, *tables],
+        5 * 2 * total * total * qw,
+        attend_backward,
+        scratch_shapes=[pltpu.VMEM((total, qw), f32), pltpu.VMEM((total, 2 * HD), f32)],
+    )[0]
+
+
+def project_out(order, values, blocks, first_col, out_type, part):
+    total, depth = values.shape
+    rows = total // 2
+    nb = order.shape[0]
+    bw = blocks[0].shape[-2]
+    whole = first_col % depth != 0
+
+    def kernel(order, v_ref, *refs):
+        w, out = views(refs[:-1]), refs[-1]
+        base = first_col if whole else 0
+        for k in range(nb):
+            acc = dot(v_ref[:, :bw], w[k][:, base : base + bw], NN)
+            for j in range(1, depth // bw):
+                acc += dot(v_ref[:, j * bw : (j + 1) * bw], w[k][:, base + j * bw : base + (j + 1) * bw], NN)
+            out[:, cols(order[k], bw)] = acc.astype(out.dtype)
+
+    return call(
+        kernel,
+        [((rows, nb * bw), out_type)],
+        [order, values, *blocks],
+        2 * rows * depth * nb * bw,
+        project_out,
+        grid=(1,),
+        in_specs=[SMEM, pl.BlockSpec((rows, depth), lambda t: (part, 0))]
+        + [block_spec(b, b.shape[-1] if whole else depth, lambda t: 0 if whole else first_col // depth) for b in blocks],
+        out_specs=[pl.BlockSpec((rows, nb * bw), lambda t: (0, 0))],
+    )[0]
+
+
+def ffn_forward(order, near, far, blocks, units):
+    rows, width = near.shape
+    nb = order.shape[0]
+    bw = width // nb
+    tile = min(256, units)
+    tiles = units // tile
+
+    def kernel(order, near, far, *refs):
+        hid, by_gate, by_up, wide = refs[-4:]
+        w = views(refs[:-4])
+        for k in range(nb):
+            wide[0, cols(order[k], bw), :] = w[k][...]
+            wide[1, cols(order[k], bw), :] = w[nb + k][...]
+        for part, a in enumerate((near, far)):
+            here = slice(part * rows, (part + 1) * rows)
+            gate = dot(a[...], wide[0], NN)
+            up = dot(a[...], wide[1], NN)
+            sigma = 1.0 / (1.0 + jnp.exp(-gate))
+            silu = gate * sigma
+            hid[here, :] = (silu * up).astype(bf16)
+            by_gate[here, :] = (up * sigma * (1.0 + gate * (1.0 - sigma))).astype(bf16)
+            by_up[here, :] = silu.astype(bf16)
+
+    all_rows = pl.BlockSpec((rows, width), lambda t: (0, 0))
+    return call(
+        kernel,
+        [((2 * rows, units), bf16)] * 3,
+        [order, near, far, *blocks, *blocks],
+        2 * 2 * rows * width * 2 * units,
+        ffn_forward,
+        grid=(tiles,),
+        in_specs=[SMEM, all_rows, all_rows]
+        + [block_spec(b, tile, lambda t: t) for b in blocks]
+        + [block_spec(b, tile, lambda t: t + tiles) for b in blocks],
+        out_specs=[pl.BlockSpec((2 * rows, tile), lambda t: (0, t))] * 3,
+        scratch_shapes=[pltpu.VMEM((2, width, tile), bf16)],
+    )
+
+
+def ffn_backward(order, near, far, by_gate, by_up, blocks):
+    rows, width = near.shape
+    nb = order.shape[0]
+    units = by_gate.shape[1]
+    bw = width // nb
+
+    def kernel(order, near, far, by_gate, by_up, *refs):
+        d_gate, d_up, wide = refs[-3:]
+        w = views(refs[:-3])
+        for k in range(nb):
+            wide[:, cols(order[k], bw)] = w[k][...]
+        for part, a in enumerate((near, far)):
+            here = slice(part * rows, (part + 1) * rows)
+            acc = dot(a[...], wide[...], NT)
+            d_gate[here, :] = (acc * by_gate[here, :].astype(f32)).astype(bf16)
+            d_up[here, :] = (acc * by_up[here, :].astype(f32)).astype(bf16)
+
+    all_rows = pl.BlockSpec((rows, width), lambda t: (0, 0))
+    tall = pl.BlockSpec((2 * rows, bw), lambda t: (0, t))
+    return call(
+        kernel,
+        [((2 * rows, units), bf16)] * 2,
+        [order, near, far, by_gate, by_up, *blocks],
+        2 * 2 * rows * width * units,
+        ffn_backward,
+        grid=(units // bw,),
+        in_specs=[SMEM, all_rows, all_rows, tall, tall]
+        + [block_spec(b, bw, lambda t: 2 * units // bw + t) for b in blocks],
+        out_specs=[tall] * 2,
+        scratch_shapes=[pltpu.VMEM((bw, width), bf16)],
+    )
+
+
+def ffn_input_grad(order, d_gate, d_up, blocks):
+    total, units = d_gate.shape
+    rows = total // 2
+    nb = order.shape[0]
+    bw = blocks[0].shape[-2]
+
+    def kernel(order, dg, du, *refs):
+        far, near, slots, sems = refs[-4:]
+        w = views(refs[:-4])
+
+        def fetch(k):
+            return pltpu.make_async_copy(w[k].at[:, : 2 * units], slots.at[k % 2], sems.at[k % 2])
+
+        fetch(0).start()
+        for k in range(nb):
+            if k + 1 < nb:
+                fetch(k + 1).start()
+            fetch(k).wait()
+            here = cols(order[k], bw)
+            for out, part in ((near, 0), (far, 1)):
+                tokens = slice(part * rows, (part + 1) * rows)
+                acc = dot(dg[tokens, :], slots[k % 2, :, :units], NT) + dot(du[tokens, :], slots[k % 2, :, units:], NT)
+                out[:, here] = acc.astype(out.dtype)
+
+    return call(
+        kernel,
+        [((rows, nb * bw), bf16), ((rows, nb * bw), f32)],
+        [order, d_gate, d_up, *blocks],
+        2 * total * 2 * units * nb * bw,
+        ffn_input_grad,
+        in_specs=[SMEM, VMEM, VMEM] + [pl.BlockSpec(memory_space=pl.ANY)] * len(blocks),
+        scratch_shapes=[pltpu.VMEM((2, bw, 2 * units), bf16), pltpu.SemaphoreType.DMA((2,))],
+    )
+
+
+def block_columns(rows, width, places):
+    return [pl.BlockSpec((rows, width), lambda t, order, p=p: (0, order[p])) for p in places for _ in range(4)]
+
+
+def turn(left, first, turned):
+    rows, width = left[0].shape
+    for p in range(len(left) // 4):
+        for part in range(2):
+            turned[p * width : (p + 1) * width, part * rows : (part + 1) * rows] = left[4 * p + first + part][...].T
+
+
+def store(out, acc, got, here=slice(None)):
+    width = out.shape[1]
+    for p in range(out.shape[0]):
+        value = acc[p * width : (p + 1) * width]
+        for r in got:
+            value += r[p, :, here].astype(f32)
+        out[p, :, here] = value.astype(bf16)
+
+
+def ffn_grad(order, near, far, d_gate, d_up, hidden, grad_near, grad_far, side, m, *received):
+    total, units = d_gate.shape
+    rows, width = near.shape
+    bw = width // order.shape[0]
+    tile = min(512, units // 2)
+    tiles = units // tile
+    steps = tiles if side else 2 * tiles
+    begin = 2 * tiles * side
+
+    def kernel(order, dg, du, h, *refs):
+        left, got, out, turned = refs[:8], refs[8:-2], refs[-2], refs[-1]
+        step = pl.program_id(0)
+        t = step + begin
+        pl.when((step == 0) & (t < 2 * tiles))(lambda: turn(left, 0, turned))
+        pl.when(t == 2 * tiles)(lambda: turn(left, 2, turned))
+        pl.when(t < tiles)(lambda: store(out, dot(turned[...], dg[...], NN), got))
+        pl.when((t >= tiles) & (t < 2 * tiles))(lambda: store(out, dot(turned[...], du[...], NN), got))
+        pl.when(t >= 2 * tiles)(lambda: store(out, dot(turned[...], h[...], NN), got))
+
+    def tall(first):
+        return pl.BlockSpec((total, tile), lambda t, order: (0, jnp.clip(t + begin - first * tiles, 0, tiles - 1)))
+
+    part = pl.BlockSpec((2, bw, tile), lambda t, order: (0, 0, t))
+    return pl.pallas_call(
+        kernel,
+        out_shape=jax.ShapeDtypeStruct((2, bw, steps * tile), bf16),
+        grid_spec=pltpu.PrefetchScalarGridSpec(
+            num_scalar_prefetch=1,
+            grid=(steps,),
+            in_specs=[tall(0), tall(1), tall(2)] + block_columns(rows, bw, (2 * m, 2 * m + 1)) + [part] * len(received),
+            out_specs=part,
+            scratch_shapes=[pltpu.VMEM((2 * bw, total), bf16)],
+        ),
+        cost_estimate=pl.CostEstimate(flops=int(4 * total * steps * tile * bw * COST_SCALE), bytes_accessed=1024, transcendentals=0),
+        compiler_params=pltpu.CompilerParams(vmem_limit_bytes=VMEM_MIB * 2**20),
+        name=ffn_grad.__name__,
+    )(order, d_gate, d_up, hidden, *([near, far, grad_near, grad_far] * 2), *received)
+
+
+def attn_grad(order, near, far, d_qkv, attended, grad_near, grad_far, m, *received):
+    total, nq = d_qkv.shape
+    rows, width = near.shape
+    bw = width // order.shape[0]
+
+    def kernel(order, dq, att, *refs):
+        left, got, out = refs[:8], refs[8:-1], refs[-1]
+        for p in range(2):
+            near, far, gn, gf = left[4 * p : 4 * p + 4]
+            value = dot(near[...], dq[:rows, :], TN) + dot(far[...], dq[rows:, :], TN)
+            for r in got:
+                value += r[p, :, :nq].astype(f32)
+            out[p, :, :nq] = value.astype(bf16)
+            value = dot(att[:rows, :], gn[...], TN) + dot(att[rows:, :], gf[...], TN)
+            for r in got:
+                value += r[p, :, nq:].astype(f32)
+            out[p, :, nq:] = value.astype(bf16)
+
+    def whole(shape):
+        return pl.BlockSpec(shape, lambda t, order: (0,) * len(shape))
+
+    shape = (2, bw, nq + bw)
+    return pl.pallas_call(
+        kernel,
+        out_shape=jax.ShapeDtypeStruct(shape, bf16),
+        grid_spec=pltpu.PrefetchScalarGridSpec(
+            num_scalar_prefetch=1,
+            grid=(1,),
+            in_specs=[whole(d_qkv.shape), whole(attended.shape)]
+            + block_columns(rows, bw, (2 * m, 2 * m + 1))
+            + [whole(shape)] * len(received),
+            out_specs=whole(shape),
+        ),
+        cost_estimate=pl.CostEstimate(flops=int(4 * total * (nq + bw) * bw * COST_SCALE), bytes_accessed=1024, transcendentals=0),
+        compiler_params=pltpu.CompilerParams(vmem_limit_bytes=VMEM_MIB * 2**20),
+        name=attn_grad.__name__,
+    )(order, d_qkv, attended, *([near, far, grad_near, grad_far] * 2), *received)
+
+
+def out_backward(order, near, far, blocks):
+    rows, width = near.shape
+    nb = order.shape[0]
+    bw = width // nb
+    qw = GROUPS * HD
+
+    def kernel(order, near, far, *refs):
+        w, out = views(refs[:-1]), refs[-1]
+        for part, a in enumerate((near, far)):
+            acc = dot(a[:, cols(order[0], bw)], w[0][:, qw + 2 * HD :], NT)
+            for k in range(1, nb):
+                acc += dot(a[:, cols(order[k], bw)], w[k][:, qw + 2 * HD :], NT)
+            out[part * rows : (part + 1) * rows, :] = acc.astype(bf16)
+
+    return call(
+        kernel, [((2 * rows, qw), bf16)], [order, near, far, *blocks], 2 * 2 * rows * width * qw, out_backward
+    )[0]
+
+
+def qkv_backward(order, d_qkv, blocks):
+    total, nq = d_qkv.shape
+    rows = total // 2
+    nb = order.shape[0]
+    bw = blocks[0].shape[-2]
+
+    def kernel(order, d_ref, *refs):
+        w, (far_out, near_out) = views(refs[:-2]), refs[-2:]
+        for k in range(nb):
+            here = cols(order[k], bw)
+            far_out[:, here] = dot(d_ref[rows:, :], w[k][:, :nq], NT).astype(bf16)
+            near_out[:, here] = dot(d_ref[:rows, :], w[k][:, :nq], NT)
+
+    return call(
+        kernel,
+        [((rows, nb * bw), bf16), ((rows, nb * bw), f32)],
+        [order, d_qkv, *blocks],
+        2 * total * nb * bw * nq,
+        qkv_backward,
+    )
+
+
+def gather_group(flow, point, n, block):
+    half = block.shape[0] // 2
+    beside, pair, far_block = flow.point(point, n, (swap_tp(block), swap_fsdp(block), swap_core(block)))
+    last = jnp.concatenate((swap_tp(pair[:half]), swap_fsdp(beside[half:])), axis=0)
+    far_pair, far_beside = swap_core(pair), swap_core(beside)
+    last, far_pair, far_beside = flow.point(point + 1, n, (last, far_pair, far_beside))
+    near = jnp.concatenate((block, beside, pair, last), axis=0)
+    return (near, jnp.concatenate((far_block, far_beside, far_pair, swap_core(last)), axis=0))
+
+
+def sum_group(flow, point, n, near, far):
+    half = far.shape[0] // 2
+    high = flow.point(point, n, near[half:] + swap_core(far[half:]).astype(f32))
+    low = near[:half] + swap_core(far[:half]).astype(f32)
+    half //= 2
+    split = half // 2
+    last = high[half:].astype(bf16)
+    by_tp, by_fsdp = flow.point(point + 1, n, (swap_tp(last[:split]), swap_fsdp(last[split:])))
+    pair = jnp.concatenate((high[:split] + by_tp.astype(f32), high[split:half]), axis=0).astype(bf16)
+    beside = jnp.concatenate((low[half : half + split], low[half + split :] + by_fsdp.astype(f32)), axis=0).astype(bf16)
+    return low[:half] + swap_tp(beside).astype(f32) + swap_fsdp(pair).astype(f32)
+
+
+def row_scale(values):
+    return lax.rsqrt(jnp.mean(values * values, axis=-1, keepdims=True) + norm_eps)
+
+
+def group_layer(flow, n, state, attn_w, gains, order, spots, start, tables):
+    scale_one = row_scale(state)
+    a_near, a_far = gather_group(flow, A_MID, n, (state * scale_one * gains[0]).astype(bf16))
+    q, kv = qkv_forward(order, spots, a_near, a_far, tables, attn_w)
+    attended, lse = attend_forward(spots, q, kv, start)
+    attended = flow.point(ATT, n, attended)
+    first_col = kv.shape[1] + q.shape[1]
+    far = project_out(order, attended, attn_w, first_col, bf16, 1)
+    near = project_out(order, attended, attn_w, first_col, f32, 0)
+    middle = flow.point(MIDDLE, n, state + sum_group(flow, S_MID, n, near, far))
+    scale_two = row_scale(middle)
+    b_near, b_far = gather_group(flow, B_MID, n, (middle * scale_two * gains[1]).astype(bf16))
+    ffn_w = [flow.get(k, n) for k in ((F0, F1, F2, F3) if n else (F0, E0, F1, E1, F2, E2, F3, E3))]
+    units = ffn_w[0].shape[-1] // 3
+    hidden, by_gate, by_up = ffn_forward(order, b_near, b_far, ffn_w, units)
+    hidden = flow.point(HIDDEN, n, hidden)
+    far = project_out(order, hidden, ffn_w, 2 * units, bf16, 1)
+    near = project_out(order, hidden, ffn_w, 2 * units, f32, 0)
+    result = flow.point(RESULT, n, middle + sum_group(flow, R_MID, n, near, far))
+    kept = (attn_w, ffn_w, state, scale_one, a_near, a_far, q, kv, attended, lse)
+    return (result, kept + (middle, scale_two, b_near, b_far, hidden, by_gate, by_up))
+
+
+def norm_back(values, scale_rows, gain, grad_normed):
+    scaled = values * scale_rows
+    grad_gain = jnp.sum(grad_normed * scaled, axis=0)
+    grad_hat = grad_normed * gain
+    grad_in = scale_rows * (grad_hat - scaled * jnp.mean(grad_hat * scaled, axis=-1, keepdims=True))
+    return (grad_in, grad_gain)
+
+
+def send_back(flow, n, makes, names):
+    last = [make(3) for make in makes]
+    for m in (2, 1, 0):
+        for k, make in enumerate(makes):
+            flow.send(names[k][2 - m], n, ring_back, last[k], True)
+        last = [make(m, flow.get(names[k][2 - m], n)) for k, make in enumerate(makes)]
+        if m:
+            yield last[0]
+    for k in range(len(makes)):
+        flow.put(names[k][3], n, swap_fsdp(last[k][1]))
+        flow.put(names[k][4], n, last[k][0])
+    yield last[0]
+
+
+def group_layer_back(flow, n, saved, grad_out, gains, order, spots, start, tables):
+    (attn_w, ffn_w, state, scale_one, a_near, a_far, q, kv, attended, lse) = saved[:10]
+    (middle, scale_two, b_near, b_far, hidden, by_gate, by_up) = saved[10:]
+    g_near, g_far = gather_group(flow, G_MID, n, grad_out.astype(bf16))
+    d_gate, d_up = ffn_backward(order, g_near, g_far, by_gate, by_up, ffn_w)
+    d_gate = flow.point(D_HID, n, d_gate)
+    makes = [partial(ffn_grad, order, b_near, b_far, d_gate, d_up, hidden, g_near, g_far, side) for side in range(2)]
+    rounds = send_back(flow, n, makes, ((G1, G2, G3, GX, FFN_SUM), (L1, L2, L3, LX, LOW_SUM)))
+    next(rounds)
+    if n:
+        next(rounds), next(rounds)
+        d_gate, _ = lax.optimization_barrier((d_gate, flow.first))
+    far, near = ffn_input_grad(order, d_gate, d_up, ffn_w)
+    grad_mid, gain_two = norm_back(middle, scale_two, gains[1], sum_group(flow, C_MID, n, near, far))
+    grad_mid = flow.point(D_MID, n, grad_mid + grad_out)
+    m_near, m_far = gather_group(flow, M_MID, n, grad_mid.astype(bf16))
+    d_att = flow.point(D_OUT, n, out_backward(order, m_near, m_far, attn_w))
+    d_qkv = flow.point(D_KEYS, n, attend_backward(spots, q, kv, lse, d_att, start, tables))
+    far, near = qkv_backward(order, d_qkv, attn_w)
+    make_attn = partial(attn_grad, order, a_near, a_far, d_qkv, attended, m_near, m_far)
+    for _ in send_back(flow, n, [make_attn], ((H1, H2, H3, HX, ATTN_SUM),)):
+        pass
+    for _ in rounds:
+        pass
+    far = flow.point(D_QKV, n, far)
+    grad_in, gain_one = norm_back(state, scale_one, gains[0], sum_group(flow, E_MID, n, near, far))
+    return (flow.point(D_IN, n, grad_mid + grad_in), (gain_one, gain_two))
+
+
+def local_group(boundary, segments, qkv_w, out_w, gate_up_w, down_w, norm_gains):
+    nz = lax.axis_size("ctx")
+    s, x, z, y = (lax.axis_index(a) for a in ("section", "fsdp", "ctx", "tp"))
+    rows, width = boundary.shape[3:]
+    own_rows = rows // 2
+
+    ends = lax.dynamic_slice_in_dim(boundary[0, :, 0], y * own_rows, own_rows, axis=1)
+
+    def moves(micro, core):
+        return [
+            ((core * 2 + f) * nz + c, (c // 2 * 2 + c % 2) * nz + 2 * micro + f) for f in range(2) for c in range(nz)
+        ]
+
+    axes = ("section", "fsdp", "ctx")
+    late = lax.div(z, 2)
+    came = [lax.ppermute(ends[t], axes, moves(t, 0)) for t in range(2)]
+    state = pick(late, came[0], came[1]).astype(f32)
+
+    g = norm_gains[0].astype(f32)
+    other = swap_core(g)
+    g = jnp.concatenate([pick(s, g, other), pick(s, other, g)], axis=0)
+    bit = 1
+    while bit < nz:
+        other = swap_ctx(g, bit)
+        side = lax.rem(lax.div(z, bit), 2)
+        g = jnp.concatenate([pick(side, g, other), pick(side, other, g)], axis=1)
+        bit *= 2
+    other = swap_fsdp(g)
+    gains = jnp.concatenate([pick(x, g, other), pick(x, other, g)], axis=1).reshape(2, 2, width)
+
+    def parts_of(cut):
+        mine, pair = cut(x, s), cut(1 - x, s)
+        got = swap_core(jnp.stack([cut(x, 1 - s), cut(1 - x, 1 - s)]))
+        return [(pick(s ^ k, mine, got[0]), pick(s ^ k, pair, got[1])) for k in range(2)]
+
+    heads = qkv_w.shape[3]
+    head_rows = out_w.shape[1] // 4
+    units = gate_up_w.shape[3] // 4
+    block = qkv_w.shape[1]
+    qkv_own = qkv_w[0].reshape(block, -1)
+
+    def cut_attn(p, c):
+        k = 2 * p + c
+        left = lax.dynamic_slice_in_dim(qkv_own, k * heads, heads, axis=1)
+        right = lax.dynamic_slice_in_dim(out_w[0], k * head_rows, head_rows, axis=0)
+        return jnp.concatenate([left, right], axis=1)
+
+    def cut_ffn(p, c):
+        k = 2 * p + c
+        gate_up = lax.dynamic_slice_in_dim(gate_up_w[0], k * units, units, axis=2)
+        down = lax.dynamic_slice_in_dim(down_w[0], k * units, units, axis=0)
+        panels = [down[j * block : (j + 1) * block] for j in range(units // block)]
+        return jnp.concatenate([gate_up[:, 0], gate_up[:, 1]] + panels, axis=1)
+
+    flow = Flow()
+
+    attn_parts = parts_of(cut_attn)
+    pairs = swap_fsdp(jnp.stack([attn_parts[n][1] for n in range(2)]))
+    line = [jnp.stack([attn_parts[0][0], pairs[0], attn_parts[1][0], pairs[1]])]
+    line[0], state = lax.optimization_barrier((line[0], state))
+    gate_up_w, down_w, first, gains = lax.optimization_barrier((gate_up_w, down_w, line[0], gains))
+    line = [first]
+    for m in range(3):
+        flow.send(A0, m, ring, line[-1])
+        line.append(flow.get(A0, m))
+    attn_w = [[v[2 * n : 2 * n + 2] for v in line] for n in range(2)]
+    ffn_parts = parts_of(cut_ffn)
+    flow.put(F0, 0, ffn_parts[0][0])
+    flow.put(E0, 0, swap_fsdp(ffn_parts[0][1]))
+    for m in range(3):
+        flow.send((F1, F2, F3)[m], 0, ring, flow.get((F0, F1, F2)[m], 0))
+        flow.send((E1, E2, E3)[m], 0, ring, flow.get((E0, E1, E2)[m], 0))
+    flow.put(F0, 1, jnp.stack([ffn_parts[1][0], swap_fsdp(ffn_parts[1][1])]))
+    for m in range(3):
+        flow.send((F1, F2, F3)[m], 1, ring, flow.get((F0, F1, F2)[m], 1))
+    ends, _ = lax.optimization_barrier((ends, flow.get(E3, 0)))
+    came = [lax.ppermute(ends[t], axes, moves(t, 1)) for t in range(2)]
+    flow.put(ENDS, 1, pick(late, came[0], came[1]))
+
+    order = jnp.stack([(x ^ i) * nz + lax.rem(z + nz - m, nz) for m in range(nz) for i in range(2)]).astype(jnp.int32)
+
+    spots = jnp.stack([(4 * s + 2 * x + y) ^ k for k in range(8)]).astype(jnp.int32)
+    batch = lax.rem(z, 2)
+    seg_here = segments[:, 0].astype(f32)
+    seg_all = pick(batch ^ x, seg_here, swap_fsdp(seg_here))
+    seg = pick(late, seg_all[0], seg_all[1])
+    start = jnp.sum((seg[None, :] < seg[:, None]).astype(jnp.int32), axis=1)
+    pos = jnp.arange(seg.shape[0], dtype=jnp.int32)
+    lane = jnp.arange(128)
+    inverse = rope_base ** (-2.0 * (lane % (HD // 2)).astype(f32) / HD)
+    angles = (pos - start).astype(f32)[:, None] * inverse[None, :]
+    cosine, sine = jnp.cos(angles), jnp.sin(angles)
+    low_half = (lane % HD) < HD // 2
+    tables = (cosine, jnp.where(low_half, -sine, 0.0), jnp.where(low_half, 0.0, sine))
+
+    start = start[:, None]
+    state, kept_0 = group_layer(flow, 0, state, attn_w[0], gains[0], order, spots, start, tables)
+    state = state.astype(bf16).astype(f32)
+    final, kept_1 = group_layer(flow, 1, state, attn_w[1], gains[1], order, spots, start, tables)
+
+    grad, gains_1 = group_layer_back(flow, 1, kept_1, flow.get(ENDS, 1).astype(f32), gains[1], order, spots, start, tables)
+    grad, gains_0 = group_layer_back(flow, 0, kept_0, grad, gains[0], order, spots, start, tables)
+    grads = [
+        [(flow.get(own, n), flow.get(pair, n)) for own, pair in ((ATTN_SUM, HX), (FFN_SUM, GX), (LOW_SUM, LX))]
+        for n in range(2)
+    ]
+    gain_grads = [gains_0, gains_1]
+
+    grad, final, _ = lax.optimization_barrier((grad, final, flow.get(L3, 0)))
+    went = [
+        [lax.ppermute(v.astype(bf16), axes, [(b, a) for a, b in moves(t, core)]) for t in range(2)]
+        for core, v in enumerate((grad, final))
+    ]
+    both = jnp.stack([pick(s, went[0][t], went[1][t]) for t in range(2)])
+    other = swap_tp(both)
+    ends_out = jnp.concatenate([pick(y, both, other), pick(y, other, both)], axis=1).astype(f32)
+
+    def settle(which):
+        (mine_0, pair_0), (mine_1, pair_1) = grads[0][which], grads[1][which]
+        mine, pair = pick(s, mine_0, mine_1), pick(s, pair_0, pair_1)
+        got = swap_core(jnp.stack([pick(s, mine_1, mine_0), pick(s, pair_1, pair_0)]))
+        first = (pick(x, mine, pair), pick(x, got[0], got[1]))
+        second = (pick(x, pair, mine), pick(x, got[1], got[0]))
+        return [pick(s ^ c, *half) for half in (first, second) for c in range(2)]
+
+    attn = settle(0)
+    grad_qkv = jnp.stack([v[:, :heads] for v in attn], axis=1).astype(f32)
+    grad_out = jnp.concatenate([v[:, heads:] for v in attn], axis=0).astype(f32)
+    ffn = settle(1)
+    grad_gate_up = jnp.stack(
+        [jnp.concatenate([v[:, t * units : (t + 1) * units] for v in ffn], axis=1) for t in range(2)], axis=1
+    ).astype(f32)
+    grad_down = jnp.concatenate(settle(2), axis=1).T.astype(f32)
+
+    g = [jnp.stack(pair) for pair in gain_grads]
+    g = pick(s, g[0], g[1]) + swap_core(pick(s, g[1], g[0]))
+
+    def fold(value, side, swap):
+        half = value.shape[1] // 2
+        first, second = value[:, :half], value[:, half:]
+        return pick(side, first, second) + swap(pick(side, second, first))
+
+    g = fold(g, x, swap_fsdp)
+    g = g + swap_tp(g)
+    g, _ = lax.optimization_barrier((g, flow.get(L3, 0)))
+    bit = nz // 2
+    while bit:
+        g = fold(g, lax.rem(lax.div(z, bit), 2), lambda v: swap_ctx(v, bit))
+        bit //= 2
+
+    return (ends_out[None, :, None], grad_qkv[None], grad_out[None], grad_gate_up[None], grad_down[None], g[0][None], g[1][None])
+
+
 def solution(mesh):
+    size = mesh.shape
+    grouped = size["section"] == size["fsdp"] == size["tp"] == 2 and size["ctx"] == 4 and KV // size["tp"] == 4
     return jax.shard_map(
-        local,
+        local_group if grouped else local,
         mesh=mesh,
         in_specs=(
             P("section", None, "fsdp", "ctx", None),

time: 3300 us -> 1370 us (0.42)
  waiting for transfers between devices: 2340 us -> 608 us
  matrix products: 623 us -> 0 us
  starting transfers between devices: 13.7 us -> 326 us
  Pallas kernels: 0 us -> 233 us
  other arithmetic: 191 us -> 82.1 us
    all_gather x7 -> x0, waiting for transfers between devices: 1030 us -> none  [the longest x1 636 us: local(): lax.all_gather(gate_up_w[0], ('fsdp', 'ctx'), axis=0, tiled=True)]
    reduce_scatter x7 -> x0, waiting for transfers between devices: 914 us -> none  [the longest x1 543 us: local(): lax.psum_scatter(totals[2].astype(jnp.bfloat16), ('fsdp', 'ctx'), scatter...]
    dot_general x57 -> x0, matrix products: 623 us -> none  [the longest x3 109 us: layer_backward(): jnp.einsum('rd,rtf->dtf', ffn_in, grad_pair_ff, preferred_element_type=jn...]
    ppermute x4 -> x175, waiting for transfers between devices: 4.71 us -> 608 us  [the longest x12 242 us: ring(): lax.ppermute(value, 'ctx', [(i, (i + 1) % size) for i in range(size)])]
    psum x9 -> x0, waiting for transfers between devices: 397 us -> none  [the longest x3 131 us: layer_forward(): lax.psum(jnp.dot(attended_low, out_full, preferred_element_type=jnp.float...]
    ppermute x4 -> x175, starting transfers between devices: 10.1 us -> 326 us  [the longest x55 118 us: swap_core(): return lax.ppermute(value, 'section', [(0, 1), (1, 0)])]
    pallas_call x0 -> x48, Pallas kernels: none -> 233 us  [the longest x24 145 us: call(): pl.pallas_call(kernel, out_shape=[jax.ShapeDtypeStruct(s, d) for s, d in...]
    convert_element_type x22 -> x14, other arithmetic: 68.5 us -> 6.9 us  [the longest x2 2.43 us: group_layer_back(): m_near, m_far = gather_group(flow, M_MID, n, grad_mid.astype(bf16))]
  transfers between devices with their start and end apart: 28 -> 175, of which waited for: 24 -> 70; matrix products, arithmetic and copies ran while one was open for 12% -> 9% of each run, Pallas kernels for 0% -> 14%
where the time goes in v1:
time: 1370 us; the launch traced here: 1360 us
  waiting for transfers between devices  608 us (44%)
  starting transfers between devices  326 us (24%)
  Pallas kernels  233 us (17%)
  local copies, waits for them, and re-layouts  108 us (8%)
  other arithmetic  82.1 us (6%)
    ppermute x12, waiting for transfers between devices, ring(): lax.ppermute(value, 'ctx', [(i, (i + 1) % size) for i in range(size)])  242 us
    ppermute x18, waiting for transfers between devices, ring_back(): lax.ppermute(value, 'ctx', [((i + 1) % size, i) for i in range(size)])  173 us
    pallas_call x24, Pallas kernels, call(): pl.pallas_call(kernel, out_shape=[jax.ShapeDtypeStruct(s, d) for s, d in...  145 us
    ppermute x55, starting transfers between devices, swap_core(): return lax.ppermute(value, 'section', [(0, 1), (1, 0)])  118 us
    ppermute x44, waiting for transfers between devices, swap_fsdp(): return lax.ppermute(value, 'fsdp', [(0, 1), (1, 0)])  101 us
    unnamed x490, local copies, waits for them, and re-layouts  79 us
    pallas_call x16, Pallas kernels, ffn_grad(): pl.pallas_call(kernel, out_shape=jax.ShapeDtypeStruct((2, bw, steps * til...  70.9 us
    ppermute x34, waiting for transfers between devices, swap_tp(): return lax.ppermute(value, 'tp', [(0, 1), (1, 0)])  65.3 us
  transfers between devices with their start and end apart: 175, of which 70 were waited for; matrix products, arithmetic and copies ran while one was open for 9% of the time, Pallas kernels for 14%

profile of v1, /device:TPU:3, one launch (start us, length us, event | category | flops | bytes accessed | tf_op | source)
XLA Modules:
  0.0 1362.1 jit_solution(10480530611721632307)
XLA Ops:
  19.9 7.7 collective-permute-done.2
  29.7 14.5 %collective-permute-done.1 = bf16[2,256,640]{2,1,0:T(8,128)(2,1)S(1)} collective-permute-done((bf16[2,256,640]{2,1,0:T(8,128)(2,1)S(1)}, bf16[2,256,640]{2,1,0:T(8,128)(2,1)S(1)}, u32[]{:S(2)}, u32[]{:S(2)}) %collective-permute-start.1) | collective-permute-done | bytes 655392 | tf_op jit(solution)/shard_map/ppermute | solution.py:382
  62.7 11.5 collective-permute-done.17
  82.5 21.0 %collective-permute-done.18 = bf16[4,256,640]{2,1,0:T(8,128)(2,1)S(1)} collective-permute-done((bf16[4,256,640]{2,1,0:T(8,128)(2,1)}, bf16[4,256,640]{2,1,0:T(8,128)(2,1)S(1)}, u32[]{:S(2)}, u32[]{:S(2)}) %collective-permute-start.18) | collective-permute-done | bytes 1310752 | tf_op jit(solution)/shard_map/ppermute | solution.py:395
  113.7 17.9 %collective-permute-done.19 = bf16[4,256,640]{2,1,0:T(8,128)(2,1)S(1)} collective-permute-done((bf16[4,256,640]{2,1,0:T(8,128)(2,1)S(1)}, bf16[4,256,640]{2,1,0:T(8,128)(2,1)S(1)}, u32[]{:S(2)}, u32[]{:S(2)}) %collective-permute-start.19) | collective-permute-done | bytes 1310752 | tf_op jit(solution)/shard_map/ppermute | solution.py:395
  154.7 10.9 collective-permute-done.36.refs_2_.refs_10_
  176.1 7.0 attend_forward.2
  189.6 8.7 collective-permute-done.37.refs_3_.refs_11_
  202.7 28.5 %collective-permute-done.38.refs_4_.refs_12_ = bf16[256,3072]{1,0:T(8,128)(2,1)S(1)} collective-permute-done((bf16[256,3072]{1,0:T(8,128)(2,1)}, bf16[256,3072]{1,0:T(8,128)(2,1)S(1)}, u32[]{:S(2)}, u32[]{:S(2)}) %collective-permute-start.38) | collective-permute-done | bytes 1572896 | tf_op jit(solution)/shard_map/ppermute | solution.py:395
  234.8 6.6 collective-permute-start.23
  246.9 17.2 %collective-permute-done.39.refs_5_.refs_13_ = bf16[256,3072]{1,0:T(8,128)(2,1)S(1)} collective-permute-done((bf16[256,3072]{1,0:T(8,128)(2,1)S(1)}, bf16[256,3072]{1,0:T(8,128)(2,1)S(1)}, u32[]{:S(2)}, u32[]{:S(2)}) %collective-permute-start.39) | collective-permute-done | bytes 1572896 | tf_op jit(solution)/shard_map/ppermute | solution.py:395
  267.4 7.2 collective-permute-done.24
  276.2 6.4 collective-permute-start.27
  282.6 15.6 %collective-permute-start.28 = (bf16[128,2048]{1,0:T(8,128)(2,1)S(1)}, bf16[128,2048]{1,0:T(8,128)(2,1)S(1)}, u32[]{:S(2)}, u32[]{:S(2)}) collective-permute-start(bf16[128,2048]{1,0:T(8,128)(2,1)S(1)} %multiply_convert_fusion.1), channel_id=1, source_target_pairs={{0,16},{16,0},{1,17},{17,1},{2,18},{18,2},{3,19},{19,3},{4,20},{20... | collective-permute-start | bytes 1572872 | tf_op jit(solution)/shard_map/ppermute | solution.py:374
  301.9 12.0 collective-permute-start.31
  331.3 15.2 %collective-permute-start.42 = (bf16[128,2048]{1,0:T(8,128)(2,1)S(1)}, bf16[128,2048]{1,0:T(8,128)(2,1)S(1)}, u32[]{:S(2)}, u32[]{:S(2)}) collective-permute-start(bf16[128,2048]{1,0:T(8,128)(2,1)S(1)} %get-tuple-element.464), channel_id=1, source_target_pairs={{16,0},{18,8},{20,16},{22,24},{24,2},{26,10},{28,18},{30,26},{17,1... | collective-permute-start | bytes 1572872 | tf_op jit(solution)/shard_map/ppermute | solution.py:1061
  346.5 8.0 collective-permute-start.43
  354.6 14.3 %ffn_forward.2 = (bf16[1024,1024]{1,0:T(8,128)(2,1)S(1)}, bf16[1024,1024]{1,0:T(8,128)(2,1)S(1)}, bf16[1024,1024]{1,0:T(8,128)(2,1)S(1)}) custom-call(s32[8]{0:T(128)S(1)} %stack.174.order, bf16[512,2048]{1,0:T(8,128)(2,1)S(1)} %pad_maximum_fusion.3.near.refs_0_.refs_4_, bf16[512,2048]{1,0:T(8,128)(2,1)S(1)} %constant_dynamic-update-slice_fusion.4.far.refs_1_.refs_5_, ...), custom_call_target="tpu_custom_call" | custom-call | flops 858993472 | bytes 1024 | tf_op jit(solution)/shard_map/ffn_forward/pallas_call | solution.py:466
  395.2 10.9 collective-permute-done.49
  407.1 40.9 %collective-permute-done.51.refs_1_.refs_5_ = bf16[2,256,3072]{2,1,0:T(8,128)(2,1)S(1)} collective-permute-done((bf16[2,256,3072]{2,1,0:T(8,128)(2,1)S(1)}, bf16[2,256,3072]{2,1,0:T(8,128)(2,1)S(1)}, u32[]{:S(2)}, u32[]{:S(2)}) %collective-permute-start.51) | collective-permute-done | bytes 3145760 | tf_op jit(solution)/shard_map/ppermute | solution.py:395
  452.9 8.1 collective-permute-done.52
  479.8 7.0 attend_forward.3
  493.5 43.2 %collective-permute-done.62.refs_2_.refs_6_ = bf16[2,256,3072]{2,1,0:T(8,128)(2,1)S(1)} collective-permute-done((bf16[2,256,3072]{2,1,0:T(8,128)(2,1)S(1)}, bf16[2,256,3072]{2,1,0:T(8,128)(2,1)S(1)}, u32[]{:S(2)}, u32[]{:S(2)}) %collective-permute-start.62) | collective-permute-done | bytes 3145760 | tf_op jit(solution)/shard_map/ppermute | solution.py:395
  588.4 38.9 %collective-permute-done.83.refs_3_.refs_7_ = bf16[2,256,3072]{2,1,0:T(8,128)(2,1)S(1)} collective-permute-done((bf16[2,256,3072]{2,1,0:T(8,128)(2,1)S(1)}, bf16[2,256,3072]{2,1,0:T(8,128)(2,1)S(1)}, u32[]{:S(2)}, u32[]{:S(2)}) %collective-permute-start.83) | collective-permute-done | bytes 3145760 | tf_op jit(solution)/shard_map/ppermute | solution.py:395
  627.3 13.4 ffn_forward.3
  643.3 8.0 ffn_backward.2
  659.1 11.8 ffn_input_grad.2
  677.1 27.0 %collective-permute-done.86.refs_8_ = bf16[2,256,2048]{2,1,0:T(8,128)(2,1)} collective-permute-done((bf16[2,256,2048]{2,1,0:T(8,128)(2,1)}, bf16[2,256,2048]{2,1,0:T(8,128)(2,1)}, u32[]{:S(2)}, u32[]{:S(2)}) %collective-permute-start.86) | collective-permute-done | bytes 2097184 | tf_op jit(solution)/shard_map/ppermute | solution.py:400
  718.1 10.6 collective-permute-done.94.refs_8_
  759.9 15.0 %collective-permute-done.100.refs_8_ = bf16[2,256,2048]{2,1,0:T(8,128)(2,1)S(1)} collective-permute-done((bf16[2,256,2048]{2,1,0:T(8,128)(2,1)S(1)}, bf16[2,256,2048]{2,1,0:T(8,128)(2,1)S(1)}, u32[]{:S(2)}, u32[]{:S(2)}) %collective-permute-start.100) | collective-permute-done | bytes 2097184 | tf_op jit(solution)/shard_map/ppermute | solution.py:400
  785.6 13.4 attend_backward.2.d_ref.dq
  822.2 6.1 collective-permute-done.104
  835.4 6.1 collective-permute-done.107
  844.9 23.4 %collective-permute-done.108.refs_8_ = bf16[2,256,2048]{2,1,0:T(8,128)(2,1)S(1)} collective-permute-done((bf16[2,256,2048]{2,1,0:T(8,128)(2,1)S(1)}, bf16[2,256,2048]{2,1,0:T(8,128)(2,1)S(1)}, u32[]{:S(2)}, u32[]{:S(2)}) %collective-permute-start.108) | collective-permute-done | bytes 2097184 | tf_op jit(solution)/shard_map/ppermute | solution.py:400
  898.2 8.3 ffn_backward.3
  908.9 6.5 collective-permute-done.118
  917.3 11.6 ffn_input_grad.3
  1016.1 6.6 collective-permute-done.152
  1060.0 13.2 attend_backward.3.d_ref.dq
  1090.0 10.2 collective-permute-done.146.refs_8_
  1153.1 27.4 %collective-permute-done.155.refs_8_ = bf16[2,256,2048]{2,1,0:T(8,128)(2,1)S(1)} collective-permute-done((bf16[2,256,2048]{2,1,0:T(8,128)(2,1)S(1)}, bf16[2,256,2048]{2,1,0:T(8,128)(2,1)S(1)}, u32[]{:S(2)}, u32[]{:S(2)}) %collective-permute-start.155) | collective-permute-done | bytes 2097184 | tf_op jit(solution)/shard_map/ppermute | solution.py:400
  1212.5 34.0 %collective-permute-done.157.refs_8_ = bf16[2,256,2048]{2,1,0:T(8,128)(2,1)S(1)} collective-permute-done((bf16[2,256,2048]{2,1,0:T(8,128)(2,1)S(1)}, bf16[2,256,2048]{2,1,0:T(8,128)(2,1)S(1)}, u32[]{:S(2)}, u32[]{:S(2)}) %collective-permute-start.157) | collective-permute-done | bytes 2097184 | tf_op jit(solution)/shard_map/ppermute | solution.py:400
  1259.5 8.6 collective-permute-done.158.refs_8_
  1268.8 15.1 %collective-permute-start.159 = (bf16[128,2048]{1,0:T(8,128)(2,1)S(1)}, bf16[128,2048]{1,0:T(8,128)(2,1)S(1)}, u32[]{:S(2)}, u32[]{:S(2)}) collective-permute-start(bf16[128,2048]{1,0:T(8,128)(2,1)S(1)} %multiply_add_fusion), channel_id=1, source_target_pairs={{0,0},{8,2},{16,4},{24,6},{2,8},{10,10},{18,12},{26,14},{1,1},{9,3... | collective-permute-start | bytes 1572872 | tf_op jit(solution)/shard_map/ppermute | solution.py:1095
  1297.9 8.0 collective-permute-start.160
  1306.4 6.1 collective-permute-done.168
  1328.8 15.6 %collective-permute-done.163 = bf16[2,128,2048]{2,1,0:T(8,128)(2,1)} collective-permute-done((bf16[2,128,2048]{2,1,0:T(8,128)(2,1)}, bf16[2,128,2048]{2,1,0:T(8,128)(2,1)}, u32[]{:S(2)}, u32[]{:S(2)}) %collective-permute-start.163) | collective-permute-done | bytes 1048608 | tf_op jit(solution)/shard_map/ppermute | solution.py:378
  1352.1 9.8 copy.44
  (1076 shorter events, 661.7 us)
Async XLA Ops:
  44.4 29.8 %collective-permute-start.17 = (bf16[4,256,640]{2,1,0:T(8,128)(2,1)S(1)}, bf16[4,256,640]{2,1,0:T(8,128)(2,1)}, u32[]{:S(2)}, u32[]{:S(2)}) collective-permute-start(bf16[4,256,640]{2,1,0:T(8,128)(2,1)S(1)} %pad_maximum_fusion.10), channel_id=1, source_target_pairs={{0,2},{2,4},{4,6},{6,0},{1,3},{3,5},{5,7},{7,1},{8,10},{10,12},{12... | collective-permute-start | bytes 3932168 | tf_op jit(solution)/shard_map/ppermute | solution.py:395
  58.2 51.5 %collective-permute-start.34 = (bf16[2,256,3072]{2,1,0:T(8,128)(2,1)}, bf16[2,256,3072]{2,1,0:T(8,128)(2,1)}, u32[]{:S(2)}, u32[]{:S(2)}) collective-permute-start(bf16[2,256,3072]{2,1,0:T(8,128)(2,1)} %pad_maximum_fusion), channel_id=1, source_target_pairs={{0,16},{16,0},{1,17},{17,1},{2,18},{18,2},{3,19},{19,3},{4,20},{20... | collective-permute-start | bytes 9437192 | tf_op jit(solution)/shard_map/ppermute | solution.py:374
  74.2 29.3 %collective-permute-start.18 = (bf16[4,256,640]{2,1,0:T(8,128)(2,1)}, bf16[4,256,640]{2,1,0:T(8,128)(2,1)S(1)}, u32[]{:S(2)}, u32[]{:S(2)}) collective-permute-start(bf16[4,256,640]{2,1,0:T(8,128)(2,1)} %collective-permute-done.17), channel_id=1, source_target_pairs={{0,2},{2,4},{4,6},{6,0},{1,3},{3,5},{5,7},{7,1},{8,10},{10,12},{12... | collective-permute-start | bytes 3932168 | tf_op jit(solution)/shard_map/ppermute | solution.py:395
  76.9 29.3 %collective-permute-start.8 = (bf16[128,2048]{1,0:T(8,128)(2,1)S(1)}, bf16[128,2048]{1,0:T(8,128)(2,1)}, u32[]{:S(2)}, u32[]{:S(2)}) collective-permute-start(bf16[128,2048]{1,0:T(8,128)(2,1)S(1)} %multiply_convert_fusion.2), channel_id=1, source_target_pairs={{0,1},{1,0},{2,3},{3,2},{4,5},{5,4},{6,7},{7,6},{8,9},{9,8},{10,11... | collective-permute-start | bytes 1572872 | tf_op jit(solution)/shard_map/ppermute | solution.py:378
  78.1 28.1 %collective-permute-start.9 = (bf16[128,2048]{1,0:T(8,128)(2,1)S(1)}, bf16[128,2048]{1,0:T(8,128)(2,1)S(1)}, u32[]{:S(2)}, u32[]{:S(2)}) collective-permute-start(bf16[128,2048]{1,0:T(8,128)(2,1)S(1)} %multiply_convert_fusion.2), channel_id=1, source_target_pairs={{0,8},{8,0},{1,9},{9,1},{2,10},{10,2},{3,11},{11,3},{4,12},{12,4},... | collective-permute-start | bytes 1572872 | tf_op jit(solution)/shard_map/ppermute | solution.py:382
  103.5 28.1 %collective-permute-start.19 = (bf16[4,256,640]{2,1,0:T(8,128)(2,1)S(1)}, bf16[4,256,640]{2,1,0:T(8,128)(2,1)S(1)}, u32[]{:S(2)}, u32[]{:S(2)}) collective-permute-start(bf16[4,256,640]{2,1,0:T(8,128)(2,1)S(1)} %collective-permute-done.18), channel_id=1, source_target_pairs={{0,2},{2,4},{4,6},{6,0},{1,3},{3,5},{5,7},{7,1},{8,10},{10,12},{12... | collective-permute-start | bytes 3932168 | tf_op jit(solution)/shard_map/ppermute | solution.py:395
  107.4 36.1 %collective-permute-start.12 = (bf16[64,2048]{1,0:T(8,128)(2,1)S(1)}, bf16[64,2048]{1,0:T(8,128)(2,1)}, u32[]{:S(2)}, u32[]{:S(2)}) collective-permute-start(bf16[64,2048]{1,0:T(8,128)(2,1)S(1)} %slice.714), channel_id=1, source_target_pairs={{0,8},{8,0},{1,9},{9,1},{2,10},{10,2},{3,11},{11,3},{4,12},{12,4},... | collective-permute-start | bytes 786440 | tf_op jit(solution)/shard_map/ppermute | solution.py:382
  113.6 41.0 %collective-permute-start.35 = (bf16[256,3072]{1,0:T(8,128)(2,1)}, bf16[256,3072]{1,0:T(8,128)(2,1)}, u32[]{:S(2)}, u32[]{:S(2)}) collective-permute-start(bf16[256,3072]{1,0:T(8,128)(2,1)} %get-tuple-element.363), channel_id=1, source_target_pairs={{0,8},{8,0},{1,9},{9,1},{2,10},{10,2},{3,11},{11,3},{4,12},{12,4},... | collective-permute-start | bytes 4718600 | tf_op jit(solution)/shard_map/ppermute | solution.py:382
  132.7 32.9 %collective-permute-start.36 = (bf16[256,3072]{1,0:T(8,128)(2,1)S(1)}, bf16[256,3072]{1,0:T(8,128)(2,1)}, u32[]{:S(2)}, u32[]{:S(2)}) collective-permute-start(bf16[256,3072]{1,0:T(8,128)(2,1)S(1)} %get-tuple-element.179.refs_0_.refs_8_), channel_id=1, source_target_pairs={{0,2},{2,4},{4,6},{6,0},{1,3},{3,5},{5,7},{7,1},{8,10},{10,12},{12... | collective-permute-start | bytes 4718600 | tf_op jit(solution)/shard_map/ppermute | solution.py:395
  165.6 32.7 %collective-permute-start.37 = (bf16[256,3072]{1,0:T(8,128)(2,1)}, bf16[256,3072]{1,0:T(8,128)(2,1)S(1)}, u32[]{:S(2)}, u32[]{:S(2)}) collective-permute-start(bf16[256,3072]{1,0:T(8,128)(2,1)} %collective-permute-done.35.refs_1_.refs_9_), channel_id=1, source_target_pairs={{0,2},{2,4},{4,6},{6,0},{1,3},{3,5},{5,7},{7,1},{8,10},{10,12},{12... | collective-permute-start | bytes 4718600 | tf_op jit(solution)/shard_map/ppermute | solution.py:395
  198.4 32.8 %collective-permute-start.38 = (bf16[256,3072]{1,0:T(8,128)(2,1)}, bf16[256,3072]{1,0:T(8,128)(2,1)S(1)}, u32[]{:S(2)}, u32[]{:S(2)}) collective-permute-start(bf16[256,3072]{1,0:T(8,128)(2,1)} %collective-permute-done.36.refs_2_.refs_10_), channel_id=1, source_target_pairs={{0,2},{2,4},{4,6},{6,0},{1,3},{3,5},{5,7},{7,1},{8,10},{10,12},{12... | collective-permute-start | bytes 4718600 | tf_op jit(solution)/shard_map/ppermute | solution.py:395
  231.2 32.8 %collective-permute-start.39 = (bf16[256,3072]{1,0:T(8,128)(2,1)S(1)}, bf16[256,3072]{1,0:T(8,128)(2,1)S(1)}, u32[]{:S(2)}, u32[]{:S(2)}) collective-permute-start(bf16[256,3072]{1,0:T(8,128)(2,1)S(1)} %collective-permute-done.37.refs_3_.refs_11_), channel_id=1, source_target_pairs={{0,2},{2,4},{4,6},{6,0},{1,3},{3,5},{5,7},{7,1},{8,10},{10,12},{12... | collective-permute-start | bytes 4718600 | tf_op jit(solution)/shard_map/ppermute | solution.py:395
  264.1 34.1 %collective-permute-start.40 = (bf16[256,3072]{1,0:T(8,128)(2,1)S(1)}, bf16[256,3072]{1,0:T(8,128)(2,1)S(1)}, u32[]{:S(2)}, u32[]{:S(2)}) collective-permute-start(bf16[256,3072]{1,0:T(8,128)(2,1)S(1)} %collective-permute-done.38.refs_4_.refs_12_), channel_id=1, source_target_pairs={{0,2},{2,4},{4,6},{6,0},{1,3},{3,5},{5,7},{7,1},{8,10},{10,12},{12... | collective-permute-start | bytes 4718600 | tf_op jit(solution)/shard_map/ppermute | solution.py:395
  275.2 26.6 %collective-permute-start.26 = (bf16[128,2048]{1,0:T(8,128)(2,1)S(1)}, bf16[128,2048]{1,0:T(8,128)(2,1)S(1)}, u32[]{:S(2)}, u32[]{:S(2)}) collective-permute-start(bf16[128,2048]{1,0:T(8,128)(2,1)S(1)} %multiply_convert_fusion.1), channel_id=1, source_target_pairs={{0,1},{1,0},{2,3},{3,2},{4,5},{5,4},{6,7},{7,6},{8,9},{9,8},{10,11... | collective-permute-start | bytes 1572872 | tf_op jit(solution)/shard_map/ppermute | solution.py:378
  298.1 33.1 %collective-permute-start.41 = (bf16[256,3072]{1,0:T(8,128)(2,1)S(1)}, bf16[256,3072]{1,0:T(8,128)(2,1)S(1)}, u32[]{:S(2)}, u32[]{:S(2)}) collective-permute-start(bf16[256,3072]{1,0:T(8,128)(2,1)S(1)} %collective-permute-done.39.refs_5_.refs_13_), channel_id=1, source_target_pairs={{0,2},{2,4},{4,6},{6,0},{1,3},{3,5},{5,7},{7,1},{8,10},{10,12},{12... | collective-permute-start | bytes 4718600 | tf_op jit(solution)/shard_map/ppermute | solution.py:395
  325.2 51.0 %collective-permute-start.50 = (bf16[256,3072]{1,0:T(8,128)(2,1)}, bf16[256,3072]{1,0:T(8,128)(2,1)S(1)}, u32[]{:S(2)}, u32[]{:S(2)}) collective-permute-start(bf16[256,3072]{1,0:T(8,128)(2,1)} %get-tuple-element.362), channel_id=1, source_target_pairs={{0,8},{8,0},{1,9},{9,1},{2,10},{10,2},{3,11},{11,3},{4,12},{12,4},... | collective-permute-start | bytes 4718600 | tf_op jit(solution)/shard_map/ppermute | solution.py:382
  326.4 28.1 %collective-permute-start.33 = (bf16[128,2048]{1,0:T(8,128)(2,1)S(1)}, bf16[128,2048]{1,0:T(8,128)(2,1)S(1)}, u32[]{:S(2)}, u32[]{:S(2)}) collective-permute-start(bf16[128,2048]{1,0:T(8,128)(2,1)S(1)} %pad_maximum_fusion.19), channel_id=1, source_target_pairs={{0,16},{16,0},{1,17},{17,1},{2,18},{18,2},{3,19},{19,3},{4,20},{20... | collective-permute-start | bytes 1572872 | tf_op jit(solution)/shard_map/ppermute | solution.py:374
  331.3 37.7 %collective-permute-start.42 = (bf16[128,2048]{1,0:T(8,128)(2,1)S(1)}, bf16[128,2048]{1,0:T(8,128)(2,1)S(1)}, u32[]{:S(2)}, u32[]{:S(2)}) collective-permute-start(bf16[128,2048]{1,0:T(8,128)(2,1)S(1)} %get-tuple-element.464), channel_id=1, source_target_pairs={{16,0},{18,8},{20,16},{22,24},{24,2},{26,10},{28,18},{30,26},{17,1... | collective-permute-start | bytes 1572872 | tf_op jit(solution)/shard_map/ppermute | solution.py:1061
  376.5 71.5 %collective-permute-start.51 = (bf16[2,256,3072]{2,1,0:T(8,128)(2,1)S(1)}, bf16[2,256,3072]{2,1,0:T(8,128)(2,1)S(1)}, u32[]{:S(2)}, u32[]{:S(2)}) collective-permute-start(bf16[2,256,3072]{2,1,0:T(8,128)(2,1)S(1)} %pad_maximum_fusion.1.refs_0_.refs_4_), channel_id=1, source_target_pairs={{0,2},{2,4},{4,6},{6,0},{1,3},{3,5},{5,7},{7,1},{8,10},{10,12},{12... | collective-permute-start | bytes 9437192 | tf_op jit(solution)/shard_map/ppermute | solution.py:395
  466.2 70.5 %collective-permute-start.62 = (bf16[2,256,3072]{2,1,0:T(8,128)(2,1)S(1)}, bf16[2,256,3072]{2,1,0:T(8,128)(2,1)S(1)}, u32[]{:S(2)}, u32[]{:S(2)}) collective-permute-start(bf16[2,256,3072]{2,1,0:T(8,128)(2,1)S(1)} %collective-permute-done.51.refs_1_.refs_5_), channel_id=1, source_target_pairs={{0,2},{2,4},{4,6},{6,0},{1,3},{3,5},{5,7},{7,1},{8,10},{10,12},{12... | collective-permute-start | bytes 9437192 | tf_op jit(solution)/shard_map/ppermute | solution.py:395
  489.2 49.4 %collective-permute-start.67 = (bf16[128,2048]{1,0:T(8,128)(2,1)S(1)}, bf16[128,2048]{1,0:T(8,128)(2,1)S(1)}, u32[]{:S(2)}, u32[]{:S(2)}) collective-permute-start(bf16[128,2048]{1,0:T(8,128)(2,1)S(1)} %broadcast_select_fusion.13), channel_id=1, source_target_pairs={{0,1},{1,0},{2,3},{3,2},{4,5},{5,4},{6,7},{7,6},{8,9},{9,8},{10,11... | collective-permute-start | bytes 1572872 | tf_op jit(solution)/shard_map/ppermute | solution.py:378
  489.4 49.2 %collective-permute-start.68 = (bf16[128,2048]{1,0:T(8,128)(2,1)S(1)}, bf16[128,2048]{1,0:T(8,128)(2,1)S(1)}, u32[]{:S(2)}, u32[]{:S(2)}) collective-permute-start(bf16[128,2048]{1,0:T(8,128)(2,1)S(1)} %broadcast_select_fusion.13), channel_id=1, source_target_pairs={{0,8},{8,0},{1,9},{9,1},{2,10},{10,2},{3,11},{11,3},{4,12},{12,4},... | collective-permute-start | bytes 1572872 | tf_op jit(solution)/shard_map/ppermute | solution.py:382
  491.3 47.3 %collective-permute-start.69 = (bf16[128,2048]{1,0:T(8,128)(2,1)S(1)}, bf16[128,2048]{1,0:T(8,128)(2,1)S(1)}, u32[]{:S(2)}, u32[]{:S(2)}) collective-permute-start(bf16[128,2048]{1,0:T(8,128)(2,1)S(1)} %broadcast_select_fusion.13), channel_id=1, source_target_pairs={{0,16},{16,0},{1,17},{17,1},{2,18},{18,2},{3,19},{19,3},{4,20},{20... | collective-permute-start | bytes 1572872 | tf_op jit(solution)/shard_map/ppermute | solution.py:374
  550.0 27.9 %collective-permute-start.74 = (bf16[128,2048]{1,0:T(8,128)(2,1)S(1)}, bf16[128,2048]{1,0:T(8,128)(2,1)S(1)}, u32[]{:S(2)}, u32[]{:S(2)}) collective-permute-start(bf16[128,2048]{1,0:T(8,128)(2,1)S(1)} %pad_maximum_fusion.25), channel_id=1, source_target_pairs={{0,16},{16,0},{1,17},{17,1},{2,18},{18,2},{3,19},{19,3},{4,20},{20... | collective-permute-start | bytes 1572872 | tf_op jit(solution)/shard_map/ppermute | solution.py:374
  555.8 71.4 %collective-permute-start.83 = (bf16[2,256,3072]{2,1,0:T(8,128)(2,1)S(1)}, bf16[2,256,3072]{2,1,0:T(8,128)(2,1)S(1)}, u32[]{:S(2)}, u32[]{:S(2)}) collective-permute-start(bf16[2,256,3072]{2,1,0:T(8,128)(2,1)S(1)} %collective-permute-done.62.refs_2_.refs_6_), channel_id=1, source_target_pairs={{0,2},{2,4},{4,6},{6,0},{1,3},{3,5},{5,7},{7,1},{8,10},{10,12},{12... | collective-permute-start | bytes 9437192 | tf_op jit(solution)/shard_map/ppermute | solution.py:395
  657.1 47.0 %collective-permute-start.86 = (bf16[2,256,2048]{2,1,0:T(8,128)(2,1)}, bf16[2,256,2048]{2,1,0:T(8,128)(2,1)}, u32[]{:S(2)}, u32[]{:S(2)}) collective-permute-start(bf16[2,256,2048]{2,1,0:T(8,128)(2,1)} %ffn_grad.16), channel_id=1, source_target_pairs={{2,0},{4,2},{6,4},{0,6},{3,1},{5,3},{7,5},{1,7},{10,8},{12,10},{14... | collective-permute-start | bytes 6291464 | tf_op jit(solution)/shard_map/ppermute | solution.py:400
  728.7 46.3 %collective-permute-start.100 = (bf16[2,256,2048]{2,1,0:T(8,128)(2,1)S(1)}, bf16[2,256,2048]{2,1,0:T(8,128)(2,1)S(1)}, u32[]{:S(2)}, u32[]{:S(2)}) collective-permute-start(bf16[2,256,2048]{2,1,0:T(8,128)(2,1)S(1)} %ffn_grad.18), channel_id=1, source_target_pairs={{2,0},{4,2},{6,4},{0,6},{3,1},{5,3},{7,5},{1,7},{10,8},{12,10},{14... | collective-permute-start | bytes 6291464 | tf_op jit(solution)/shard_map/ppermute | solution.py:400
  776.3 30.9 %collective-permute-start.101 = (bf16[2,256,1024]{2,1,0:T(8,128)(2,1)S(1)}, bf16[2,256,1024]{2,1,0:T(8,128)(2,1)S(1)}, u32[]{:S(2)}, u32[]{:S(2)}) collective-permute-start(bf16[2,256,1024]{2,1,0:T(8,128)(2,1)S(1)} %ffn_grad.19), channel_id=1, source_target_pairs={{2,0},{4,2},{6,4},{0,6},{3,1},{5,3},{7,5},{1,7},{10,8},{12,10},{14... | collective-permute-start | bytes 3145736 | tf_op jit(solution)/shard_map/ppermute | solution.py:400
  822.1 46.2 %collective-permute-start.108 = (bf16[2,256,2048]{2,1,0:T(8,128)(2,1)S(1)}, bf16[2,256,2048]{2,1,0:T(8,128)(2,1)S(1)}, u32[]{:S(2)}, u32[]{:S(2)}) collective-permute-start(bf16[2,256,2048]{2,1,0:T(8,128)(2,1)S(1)} %ffn_grad.20), channel_id=1, source_target_pairs={{2,0},{4,2},{6,4},{0,6},{3,1},{5,3},{7,5},{1,7},{10,8},{12,10},{14... | collective-permute-start | bytes 6291464 | tf_op jit(solution)/shard_map/ppermute | solution.py:400
  874.9 33.0 %collective-permute-start.117 = (bf16[2,256,1024]{2,1,0:T(8,128)(2,1)S(1)}, bf16[2,256,1024]{2,1,0:T(8,128)(2,1)S(1)}, u32[]{:S(2)}, u32[]{:S(2)}) collective-permute-start(bf16[2,256,1024]{2,1,0:T(8,128)(2,1)S(1)} %ffn_grad.21), channel_id=1, source_target_pairs={{2,0},{4,2},{6,4},{0,6},{3,1},{5,3},{7,5},{1,7},{10,8},{12,10},{14... | collective-permute-start | bytes 3145736 | tf_op jit(solution)/shard_map/ppermute | solution.py:400
  932.1 25.9 %collective-permute-start.120 = (bf16[256,2048]{1,0:T(8,128)(2,1)}, bf16[256,2048]{1,0:T(8,128)(2,1)}, u32[]{:S(2)}, u32[]{:S(2)}) collective-permute-start(bf16[256,2048]{1,0:T(8,128)(2,1)} %get-tuple-element.394), channel_id=1, source_target_pairs={{0,16},{16,0},{1,17},{17,1},{2,18},{18,2},{3,19},{19,3},{4,20},{20... | collective-permute-start | bytes 3145736 | tf_op jit(solution)/shard_map/ppermute | solution.py:374
  982.0 32.1 %collective-permute-start.151 = (bf16[64,2048]{1,0:T(8,128)(2,1)S(1)}, bf16[64,2048]{1,0:T(8,128)(2,1)}, u32[]{:S(2)}, u32[]{:S(2)}) collective-permute-start(bf16[64,2048]{1,0:T(8,128)(2,1)S(1)} %get-tuple-element.444), channel_id=1, source_target_pairs={{0,1},{1,0},{2,3},{3,2},{4,5},{5,4},{6,7},{7,6},{8,9},{9,8},{10,11... | collective-permute-start | bytes 786440 | tf_op jit(solution)/shard_map/ppermute | solution.py:378
  996.4 52.5 %collective-permute-start.137 = (bf16[2,256,2048]{2,1,0:T(8,128)(2,1)}, bf16[2,256,2048]{2,1,0:T(8,128)(2,1)}, u32[]{:S(2)}, u32[]{:S(2)}) collective-permute-start(bf16[2,256,2048]{2,1,0:T(8,128)(2,1)} %ffn_grad.24), channel_id=1, source_target_pairs={{2,0},{4,2},{6,4},{0,6},{3,1},{5,3},{7,5},{1,7},{10,8},{12,10},{14... | collective-permute-start | bytes 6291464 | tf_op jit(solution)/shard_map/ppermute | solution.py:400
  1007.7 29.8 %collective-permute-start.129 = (bf16[128,2048]{1,0:T(8,128)(2,1)}, bf16[128,2048]{1,0:T(8,128)(2,1)}, u32[]{:S(2)}, u32[]{:S(2)}) collective-permute-start(bf16[128,2048]{1,0:T(8,128)(2,1)} %convert_element_type.336), channel_id=1, source_target_pairs={{0,1},{1,0},{2,3},{3,2},{4,5},{5,4},{6,7},{7,6},{8,9},{9,8},{10,11... | collective-permute-start | bytes 1572872 | tf_op jit(solution)/shard_map/ppermute | solution.py:378
  1008.0 29.5 %collective-permute-start.130 = (bf16[128,2048]{1,0:T(8,128)(2,1)}, bf16[128,2048]{1,0:T(8,128)(2,1)}, u32[]{:S(2)}, u32[]{:S(2)}) collective-permute-start(bf16[128,2048]{1,0:T(8,128)(2,1)} %convert_element_type.336), channel_id=1, source_target_pairs={{0,8},{8,0},{1,9},{9,1},{2,10},{10,2},{3,11},{11,3},{4,12},{12,4},... | collective-permute-start | bytes 1572872 | tf_op jit(solution)/shard_map/ppermute | solution.py:382
  1009.2 28.3 %collective-permute-start.131 = (bf16[128,2048]{1,0:T(8,128)(2,1)}, bf16[128,2048]{1,0:T(8,128)(2,1)}, u32[]{:S(2)}, u32[]{:S(2)}) collective-permute-start(bf16[128,2048]{1,0:T(8,128)(2,1)} %convert_element_type.336), channel_id=1, source_target_pairs={{0,16},{16,0},{1,17},{17,1},{2,18},{18,2},{3,19},{19,3},{4,20},{20... | collective-permute-start | bytes 1572872 | tf_op jit(solution)/shard_map/ppermute | solution.py:374
  1078.7 27.0 %collective-permute-start.141 = (bf16[256,2048]{1,0:T(8,128)(2,1)S(1)}, bf16[256,2048]{1,0:T(8,128)(2,1)S(1)}, u32[]{:S(2)}, u32[]{:S(2)}) collective-permute-start(bf16[256,2048]{1,0:T(8,128)(2,1)S(1)} %get-tuple-element.392), channel_id=1, source_target_pairs={{0,16},{16,0},{1,17},{17,1},{2,18},{18,2},{3,19},{19,3},{4,20},{20... | collective-permute-start | bytes 3145736 | tf_op jit(solution)/shard_map/ppermute | solution.py:374
  1087.7 51.6 %collective-permute-start.154 = (bf16[128,2048]{1,0:T(8,128)(2,1)}, bf16[128,2048]{1,0:T(8,128)(2,1)}, u32[]{:S(2)}, u32[]{:S(2)}) collective-permute-start(bf16[128,2048]{1,0:T(8,128)(2,1)} %pad_maximum_fusion.39), channel_id=1, source_target_pairs={{0,8},{8,0},{1,9},{9,1},{2,10},{10,2},{3,11},{11,3},{4,12},{12,4},... | collective-permute-start | bytes 1572872 | tf_op jit(solution)/shard_map/ppermute | solution.py:382
  1112.0 27.3 %collective-permute-start.153 = (bf16[128,2048]{1,0:T(8,128)(2,1)}, bf16[128,2048]{1,0:T(8,128)(2,1)}, u32[]{:S(2)}, u32[]{:S(2)}) collective-permute-start(bf16[128,2048]{1,0:T(8,128)(2,1)} %pad_maximum_fusion.38), channel_id=1, source_target_pairs={{0,1},{1,0},{2,3},{3,2},{4,5},{5,4},{6,7},{7,6},{8,9},{9,8},{10,11... | collective-permute-start | bytes 1572872 | tf_op jit(solution)/shard_map/ppermute | solution.py:378
  1134.9 45.7 %collective-permute-start.155 = (bf16[2,256,2048]{2,1,0:T(8,128)(2,1)S(1)}, bf16[2,256,2048]{2,1,0:T(8,128)(2,1)S(1)}, u32[]{:S(2)}, u32[]{:S(2)}) collective-permute-start(bf16[2,256,2048]{2,1,0:T(8,128)(2,1)S(1)} %ffn_grad.26), channel_id=1, source_target_pairs={{2,0},{4,2},{6,4},{0,6},{3,1},{5,3},{7,5},{1,7},{10,8},{12,10},{14... | collective-permute-start | bytes 6291464 | tf_op jit(solution)/shard_map/ppermute | solution.py:400
  1151.4 33.1 %collective-permute-start.164 = (bf16[256,640]{1,0:T(8,128)(2,1)S(1)}, bf16[256,640]{1,0:T(8,128)(2,1)S(1)}, u32[]{:S(2)}, u32[]{:S(2)}) collective-permute-start(bf16[256,640]{1,0:T(8,128)(2,1)S(1)} %get-tuple-element.479), channel_id=1, source_target_pairs={{0,8},{8,0},{1,9},{9,1},{2,10},{10,2},{3,11},{11,3},{4,12},{12,4},... | collective-permute-start | bytes 983048 | tf_op jit(solution)/shard_map/ppermute | solution.py:382
  1152.7 36.9 %collective-permute-start.171 = (f32[2,1024]{1,0:T(2,128)S(1)}, f32[2,1024]{1,0:T(2,128)S(1)}, u32[]{:S(2)}, u32[]{:S(2)}) collective-permute-start(f32[2,1024]{1,0:T(2,128)S(1)} %broadcast_select_fusion.24), channel_id=1, source_target_pairs={{0,8},{8,0},{1,9},{9,1},{2,10},{10,2},{3,11},{11,3},{4,12},{12,4},... | collective-permute-start | bytes 24584 | tf_op jit(solution)/shard_map/ppermute | solution.py:382
  1202.4 44.1 %collective-permute-start.157 = (bf16[2,256,2048]{2,1,0:T(8,128)(2,1)S(1)}, bf16[2,256,2048]{2,1,0:T(8,128)(2,1)S(1)}, u32[]{:S(2)}, u32[]{:S(2)}) collective-permute-start(bf16[2,256,2048]{2,1,0:T(8,128)(2,1)S(1)} %ffn_grad.29), channel_id=1, source_target_pairs={{2,0},{4,2},{6,4},{0,6},{3,1},{5,3},{7,5},{1,7},{10,8},{12,10},{14... | collective-permute-start | bytes 6291464 | tf_op jit(solution)/shard_map/ppermute | solution.py:400
  1257.3 31.5 %collective-permute-start.166 = (bf16[256,2048]{1,0:T(8,128)(2,1)S(1)}, bf16[256,2048]{1,0:T(8,128)(2,1)S(1)}, u32[]{:S(2)}, u32[]{:S(2)}) collective-permute-start(bf16[256,2048]{1,0:T(8,128)(2,1)S(1)} %get-tuple-element.386), channel_id=1, source_target_pairs={{0,8},{8,0},{1,9},{9,1},{2,10},{10,2},{3,11},{11,3},{4,12},{12,4},... | collective-permute-start | bytes 3145736 | tf_op jit(solution)/shard_map/ppermute | solution.py:382
  1268.1 44.6 %collective-permute-start.161 = (bf16[128,2048]{1,0:T(8,128)(2,1)S(1)}, bf16[128,2048]{1,0:T(8,128)(2,1)S(1)}, u32[]{:S(2)}, u32[]{:S(2)}) collective-permute-start(bf16[128,2048]{1,0:T(8,128)(2,1)S(1)} %multiply_add_fusion), channel_id=1, source_target_pairs={{4,0},{12,2},{20,4},{28,6},{6,8},{14,10},{22,12},{30,14},{5,1},{13... | collective-permute-start | bytes 1572872 | tf_op jit(solution)/shard_map/ppermute | solution.py:1095
  1268.8 44.5 %collective-permute-start.159 = (bf16[128,2048]{1,0:T(8,128)(2,1)S(1)}, bf16[128,2048]{1,0:T(8,128)(2,1)S(1)}, u32[]{:S(2)}, u32[]{:S(2)}) collective-permute-start(bf16[128,2048]{1,0:T(8,128)(2,1)S(1)} %multiply_add_fusion), channel_id=1, source_target_pairs={{0,0},{8,2},{16,4},{24,6},{2,8},{10,10},{18,12},{26,14},{1,1},{9,3... | collective-permute-start | bytes 1572872 | tf_op jit(solution)/shard_map/ppermute | solution.py:1095
  1283.9 29.3 %collective-permute-start.162 = (bf16[128,2048]{1,0:T(8,128)(2,1)S(1)}, bf16[128,2048]{1,0:T(8,128)(2,1)S(1)}, u32[]{:S(2)}, u32[]{:S(2)}) collective-permute-start(bf16[128,2048]{1,0:T(8,128)(2,1)S(1)} %copy-done.206), channel_id=1, source_target_pairs={{4,16},{12,18},{20,20},{28,22},{6,24},{14,26},{22,28},{30,30},{5,1... | collective-permute-start | bytes 1572872 | tf_op jit(solution)/shard_map/ppermute | solution.py:1095
  1312.5 36.0 %collective-permute-start.167 = (bf16[2,256,2048]{2,1,0:T(8,128)(2,1)}, bf16[2,256,2048]{2,1,0:T(8,128)(2,1)S(1)}, u32[]{:S(2)}, u32[]{:S(2)}) collective-permute-start(bf16[2,256,2048]{2,1,0:T(8,128)(2,1)} %pad_maximum_fusion.9), channel_id=1, source_target_pairs={{0,16},{16,0},{1,17},{17,1},{2,18},{18,2},{3,19},{19,3},{4,20},{20... | collective-permute-start | bytes 6291464 | tf_op jit(solution)/shard_map/ppermute | solution.py:374
  (348 other events, 7048.2 us)

commit v2 on v1

--- a/solution.py
+++ b/solution.py
@@ -1090,7 +1090,23 @@
     ]
     gain_grads = [gains_0, gains_1]
 
-    grad, final, _ = lax.optimization_barrier((grad, final, flow.get(L3, 0)))
+    g = [jnp.stack(pair) for pair in gain_grads]
+    g = pick(s, g[0], g[1]) + swap_core(pick(s, g[1], g[0]))
+
+    def fold(value, side, swap):
+        half = value.shape[1] // 2
+        first, second = value[:, :half], value[:, half:]
+        return pick(side, first, second) + swap(pick(side, second, first))
+
+    g = fold(g, x, swap_fsdp)
+    g = g + swap_tp(g)
+    g, _ = lax.optimization_barrier((g, flow.get(L3, 0)))
+    bit = nz // 2
+    while bit:
+        g = fold(g, lax.rem(lax.div(z, bit), 2), lambda v: swap_ctx(v, bit))
+        bit //= 2
+
+    grad, final, g = lax.optimization_barrier((grad, final, g))
     went = [
         [lax.ppermute(v.astype(bf16), axes, [(b, a) for a, b in moves(t, core)]) for t in range(2)]
         for core, v in enumerate((grad, final))
@@ -1115,22 +1131,6 @@
         [jnp.concatenate([v[:, t * units : (t + 1) * units] for v in ffn], axis=1) for t in range(2)], axis=1
     ).astype(f32)
     grad_down = jnp.concatenate(settle(2), axis=1).T.astype(f32)
-
-    g = [jnp.stack(pair) for pair in gain_grads]
-    g = pick(s, g[0], g[1]) + swap_core(pick(s, g[1], g[0]))
-
-    def fold(value, side, swap):
-        half = value.shape[1] // 2
-        first, second = value[:, :half], value[:, half:]
-        return pick(side, first, second) + swap(pick(side, second, first))
-
-    g = fold(g, x, swap_fsdp)
-    g = g + swap_tp(g)
-    g, _ = lax.optimization_barrier((g, flow.get(L3, 0)))
-    bit = nz // 2
-    while bit:
-        g = fold(g, lax.rem(lax.div(z, bit), 2), lambda v: swap_ctx(v, bit))
-        bit //= 2
 
     return (ends_out[None, :, None], grad_qkv[None], grad_out[None], grad_gate_up[None], grad_down[None], g[0][None], g[1][None])
 

time: 1370 us -> 1380 us (level)
    ppermute x55, starting transfers between devices: 118 us -> 136 us  [swap_core(): return lax.ppermute(value, 'section', [(0, 1), (1, 0)])]
    ppermute x4, waiting for transfers between devices: 4.79 us -> 20.8 us  [local_group(): lax.ppermute(v.astype(bf16), axes, [(b, a) for a, b in moves(t, core)])]
  transfers between devices with their start and end apart: 175 -> 175, of which waited for: 70 -> 68; matrix products, arithmetic and copies ran while one was open for 9% -> 9% of each run, Pallas kernels for 14% -> 14%
where the time goes in v2:
time: 1380 us; the launch traced here: 1370 us
  waiting for transfers between devices  608 us (44%)
  starting transfers between devices  338 us (24%)
  Pallas kernels  233 us (17%)
  local copies, waits for them, and re-layouts  107 us (8%)
  other arithmetic  82 us (6%)
    ppermute x12, waiting for transfers between devices, ring(): lax.ppermute(value, 'ctx', [(i, (i + 1) % size) for i in range(size)])  242 us
    ppermute x18, waiting for transfers between devices, ring_back(): lax.ppermute(value, 'ctx', [((i + 1) % size, i) for i in range(size)])  173 us
    pallas_call x24, Pallas kernels, call(): pl.pallas_call(kernel, out_shape=[jax.ShapeDtypeStruct(s, d) for s, d in...  145 us
    ppermute x55, starting transfers between devices, swap_core(): return lax.ppermute(value, 'section', [(0, 1), (1, 0)])  136 us
    ppermute x44, waiting for transfers between devices, swap_fsdp(): return lax.ppermute(value, 'fsdp', [(0, 1), (1, 0)])  95.1 us
    unnamed x490, local copies, waits for them, and re-layouts  77.9 us
    pallas_call x16, Pallas kernels, ffn_grad(): pl.pallas_call(kernel, out_shape=jax.ShapeDtypeStruct((2, bw, steps * til...  70.9 us
    ppermute x34, waiting for transfers between devices, swap_tp(): return lax.ppermute(value, 'tp', [(0, 1), (1, 0)])  60.9 us
  transfers between devices with their start and end apart: 175, of which 68 were waited for; matrix products, arithmetic and copies ran while one was open for 9% of the time, Pallas kernels for 14%

profile of v2, /device:TPU:3, one launch (start us, length us, event | category | flops | bytes accessed | tf_op | source)
XLA Modules:
  0.0 1372.1 jit_solution(651387649491296592)
XLA Ops:
  19.9 7.7 collective-permute-done.2
  29.7 14.5 %collective-permute-done.1 = bf16[2,256,640]{2,1,0:T(8,128)(2,1)S(1)} collective-permute-done((bf16[2,256,640]{2,1,0:T(8,128)(2,1)S(1)}, bf16[2,256,640]{2,1,0:T(8,128)(2,1)S(1)}, u32[]{:S(2)}, u32[]{:S(2)}) %collective-permute-start.1) | collective-permute-done | bytes 655392 | tf_op jit(solution)/shard_map/ppermute | solution.py:382
  62.7 11.5 collective-permute-done.17
  82.5 21.0 %collective-permute-done.18 = bf16[4,256,640]{2,1,0:T(8,128)(2,1)S(1)} collective-permute-done((bf16[4,256,640]{2,1,0:T(8,128)(2,1)}, bf16[4,256,640]{2,1,0:T(8,128)(2,1)S(1)}, u32[]{:S(2)}, u32[]{:S(2)}) %collective-permute-start.18) | collective-permute-done | bytes 1310752 | tf_op jit(solution)/shard_map/ppermute | solution.py:395
  113.7 17.9 %collective-permute-done.19 = bf16[4,256,640]{2,1,0:T(8,128)(2,1)S(1)} collective-permute-done((bf16[4,256,640]{2,1,0:T(8,128)(2,1)S(1)}, bf16[4,256,640]{2,1,0:T(8,128)(2,1)S(1)}, u32[]{:S(2)}, u32[]{:S(2)}) %collective-permute-start.19) | collective-permute-done | bytes 1310752 | tf_op jit(solution)/shard_map/ppermute | solution.py:395
  154.7 10.9 collective-permute-done.36.refs_2_.refs_10_
  176.1 7.0 attend_forward.2
  189.6 8.7 collective-permute-done.37.refs_3_.refs_11_
  202.7 28.5 %collective-permute-done.38.refs_4_.refs_12_ = bf16[256,3072]{1,0:T(8,128)(2,1)S(1)} collective-permute-done((bf16[256,3072]{1,0:T(8,128)(2,1)}, bf16[256,3072]{1,0:T(8,128)(2,1)S(1)}, u32[]{:S(2)}, u32[]{:S(2)}) %collective-permute-start.38) | collective-permute-done | bytes 1572896 | tf_op jit(solution)/shard_map/ppermute | solution.py:395
  234.8 6.6 collective-permute-start.23
  246.9 17.2 %collective-permute-done.39.refs_5_.refs_13_ = bf16[256,3072]{1,0:T(8,128)(2,1)S(1)} collective-permute-done((bf16[256,3072]{1,0:T(8,128)(2,1)S(1)}, bf16[256,3072]{1,0:T(8,128)(2,1)S(1)}, u32[]{:S(2)}, u32[]{:S(2)}) %collective-permute-start.39) | collective-permute-done | bytes 1572896 | tf_op jit(solution)/shard_map/ppermute | solution.py:395
  267.4 7.2 collective-permute-done.24
  276.2 6.4 collective-permute-start.27
  282.6 15.6 %collective-permute-start.28 = (bf16[128,2048]{1,0:T(8,128)(2,1)S(1)}, bf16[128,2048]{1,0:T(8,128)(2,1)S(1)}, u32[]{:S(2)}, u32[]{:S(2)}) collective-permute-start(bf16[128,2048]{1,0:T(8,128)(2,1)S(1)} %multiply_convert_fusion.1), channel_id=1, source_target_pairs={{0,16},{16,0},{1,17},{17,1},{2,18},{18,2},{3,19},{19,3},{4,20},{20... | collective-permute-start | bytes 1572872 | tf_op jit(solution)/shard_map/ppermute | solution.py:374
  301.9 12.0 collective-permute-start.31
  331.3 15.2 %collective-permute-start.42 = (bf16[128,2048]{1,0:T(8,128)(2,1)S(1)}, bf16[128,2048]{1,0:T(8,128)(2,1)S(1)}, u32[]{:S(2)}, u32[]{:S(2)}) collective-permute-start(bf16[128,2048]{1,0:T(8,128)(2,1)S(1)} %get-tuple-element.466), channel_id=1, source_target_pairs={{16,0},{18,8},{20,16},{22,24},{24,2},{26,10},{28,18},{30,26},{17,1... | collective-permute-start | bytes 1572872 | tf_op jit(solution)/shard_map/ppermute | solution.py:1061
  346.5 8.0 collective-permute-start.43
  354.6 14.3 %ffn_forward.2 = (bf16[1024,1024]{1,0:T(8,128)(2,1)S(1)}, bf16[1024,1024]{1,0:T(8,128)(2,1)S(1)}, bf16[1024,1024]{1,0:T(8,128)(2,1)S(1)}) custom-call(s32[8]{0:T(128)S(1)} %stack.174.order, bf16[512,2048]{1,0:T(8,128)(2,1)S(1)} %pad_maximum_fusion.3.near.refs_0_.refs_4_, bf16[512,2048]{1,0:T(8,128)(2,1)S(1)} %constant_dynamic-update-slice_fusion.4.far.refs_1_.refs_5_, ...), custom_call_target="tpu_custom_call" | custom-call | flops 858993472 | bytes 1024 | tf_op jit(solution)/shard_map/ffn_forward/pallas_call | solution.py:466
  395.2 10.9 collective-permute-done.49
  407.1 40.9 %collective-permute-done.51.refs_1_.refs_5_ = bf16[2,256,3072]{2,1,0:T(8,128)(2,1)S(1)} collective-permute-done((bf16[2,256,3072]{2,1,0:T(8,128)(2,1)S(1)}, bf16[2,256,3072]{2,1,0:T(8,128)(2,1)S(1)}, u32[]{:S(2)}, u32[]{:S(2)}) %collective-permute-start.51) | collective-permute-done | bytes 3145760 | tf_op jit(solution)/shard_map/ppermute | solution.py:395
  452.9 8.1 collective-permute-done.52
  479.8 7.0 attend_forward.3
  493.5 43.2 %collective-permute-done.62.refs_2_.refs_6_ = bf16[2,256,3072]{2,1,0:T(8,128)(2,1)S(1)} collective-permute-done((bf16[2,256,3072]{2,1,0:T(8,128)(2,1)S(1)}, bf16[2,256,3072]{2,1,0:T(8,128)(2,1)S(1)}, u32[]{:S(2)}, u32[]{:S(2)}) %collective-permute-start.62) | collective-permute-done | bytes 3145760 | tf_op jit(solution)/shard_map/ppermute | solution.py:395
  588.4 38.9 %collective-permute-done.83.refs_3_.refs_7_ = bf16[2,256,3072]{2,1,0:T(8,128)(2,1)S(1)} collective-permute-done((bf16[2,256,3072]{2,1,0:T(8,128)(2,1)S(1)}, bf16[2,256,3072]{2,1,0:T(8,128)(2,1)S(1)}, u32[]{:S(2)}, u32[]{:S(2)}) %collective-permute-start.83) | collective-permute-done | bytes 3145760 | tf_op jit(solution)/shard_map/ppermute | solution.py:395
  627.3 13.4 ffn_forward.3
  643.3 8.0 ffn_backward.2
  659.1 11.8 ffn_input_grad.2
  677.1 27.0 %collective-permute-done.86.refs_8_ = bf16[2,256,2048]{2,1,0:T(8,128)(2,1)} collective-permute-done((bf16[2,256,2048]{2,1,0:T(8,128)(2,1)}, bf16[2,256,2048]{2,1,0:T(8,128)(2,1)}, u32[]{:S(2)}, u32[]{:S(2)}) %collective-permute-start.86) | collective-permute-done | bytes 2097184 | tf_op jit(solution)/shard_map/ppermute | solution.py:400
  718.1 10.6 collective-permute-done.94.refs_8_
  759.9 15.0 %collective-permute-done.100.refs_8_ = bf16[2,256,2048]{2,1,0:T(8,128)(2,1)S(1)} collective-permute-done((bf16[2,256,2048]{2,1,0:T(8,128)(2,1)S(1)}, bf16[2,256,2048]{2,1,0:T(8,128)(2,1)S(1)}, u32[]{:S(2)}, u32[]{:S(2)}) %collective-permute-start.100) | collective-permute-done | bytes 2097184 | tf_op jit(solution)/shard_map/ppermute | solution.py:400
  785.6 13.4 attend_backward.2.d_ref.dq
  835.4 6.1 collective-permute-done.107
  844.9 23.4 %collective-permute-done.108.refs_8_ = bf16[2,256,2048]{2,1,0:T(8,128)(2,1)S(1)} collective-permute-done((bf16[2,256,2048]{2,1,0:T(8,128)(2,1)S(1)}, bf16[2,256,2048]{2,1,0:T(8,128)(2,1)S(1)}, u32[]{:S(2)}, u32[]{:S(2)}) %collective-permute-start.108) | collective-permute-done | bytes 2097184 | tf_op jit(solution)/shard_map/ppermute | solution.py:400
  898.2 8.3 ffn_backward.3
  908.9 6.5 collective-permute-done.118
  917.3 11.6 ffn_input_grad.3
  1016.1 6.6 collective-permute-done.152
  1060.0 13.2 attend_backward.3.d_ref.dq
  1090.0 10.2 collective-permute-done.146.refs_8_
  1153.1 27.4 %collective-permute-done.158.refs_8_ = bf16[2,256,2048]{2,1,0:T(8,128)(2,1)S(1)} collective-permute-done((bf16[2,256,2048]{2,1,0:T(8,128)(2,1)S(1)}, bf16[2,256,2048]{2,1,0:T(8,128)(2,1)S(1)}, u32[]{:S(2)}, u32[]{:S(2)}) %collective-permute-start.158) | collective-permute-done | bytes 2097184 | tf_op jit(solution)/shard_map/ppermute | solution.py:400
  1212.5 34.0 %collective-permute-done.160.refs_8_ = bf16[2,256,2048]{2,1,0:T(8,128)(2,1)S(1)} collective-permute-done((bf16[2,256,2048]{2,1,0:T(8,128)(2,1)S(1)}, bf16[2,256,2048]{2,1,0:T(8,128)(2,1)S(1)}, u32[]{:S(2)}, u32[]{:S(2)}) %collective-permute-start.160) | collective-permute-done | bytes 2097184 | tf_op jit(solution)/shard_map/ppermute | solution.py:400
  1259.5 8.6 collective-permute-done.161.refs_8_
  1278.9 11.4 collective-permute-start.172
  1291.0 9.5 collective-permute-start.164
  1304.5 7.2 collective-permute-start.174
  1316.7 15.8 %collective-permute-done.165 = bf16[128,2048]{1,0:T(8,128)(2,1)S(1)} collective-permute-done((bf16[128,2048]{1,0:T(8,128)(2,1)S(1)}, bf16[128,2048]{1,0:T(8,128)(2,1)S(1)}, u32[]{:S(2)}, u32[]{:S(2)}) %collective-permute-start.165) | collective-permute-done | bytes 524320 | tf_op jit(solution)/shard_map/ppermute | solution.py:1111
  1343.2 11.1 collective-permute-done.168
  1362.0 9.8 copy.44
  (1076 shorter events, 667.4 us)
Async XLA Ops:
  44.4 29.8 %collective-permute-start.17 = (bf16[4,256,640]{2,1,0:T(8,128)(2,1)S(1)}, bf16[4,256,640]{2,1,0:T(8,128)(2,1)}, u32[]{:S(2)}, u32[]{:S(2)}) collective-permute-start(bf16[4,256,640]{2,1,0:T(8,128)(2,1)S(1)} %pad_maximum_fusion.10), channel_id=1, source_target_pairs={{0,2},{2,4},{4,6},{6,0},{1,3},{3,5},{5,7},{7,1},{8,10},{10,12},{12... | collective-permute-start | bytes 3932168 | tf_op jit(solution)/shard_map/ppermute | solution.py:395
  58.2 51.5 %collective-permute-start.34 = (bf16[2,256,3072]{2,1,0:T(8,128)(2,1)}, bf16[2,256,3072]{2,1,0:T(8,128)(2,1)}, u32[]{:S(2)}, u32[]{:S(2)}) collective-permute-start(bf16[2,256,3072]{2,1,0:T(8,128)(2,1)} %pad_maximum_fusion), channel_id=1, source_target_pairs={{0,16},{16,0},{1,17},{17,1},{2,18},{18,2},{3,19},{19,3},{4,20},{20... | collective-permute-start | bytes 9437192 | tf_op jit(solution)/shard_map/ppermute | solution.py:374
  74.2 29.3 %collective-permute-start.18 = (bf16[4,256,640]{2,1,0:T(8,128)(2,1)}, bf16[4,256,640]{2,1,0:T(8,128)(2,1)S(1)}, u32[]{:S(2)}, u32[]{:S(2)}) collective-permute-start(bf16[4,256,640]{2,1,0:T(8,128)(2,1)} %collective-permute-done.17), channel_id=1, source_target_pairs={{0,2},{2,4},{4,6},{6,0},{1,3},{3,5},{5,7},{7,1},{8,10},{10,12},{12... | collective-permute-start | bytes 3932168 | tf_op jit(solution)/shard_map/ppermute | solution.py:395
  76.9 29.3 %collective-permute-start.8 = (bf16[128,2048]{1,0:T(8,128)(2,1)S(1)}, bf16[128,2048]{1,0:T(8,128)(2,1)}, u32[]{:S(2)}, u32[]{:S(2)}) collective-permute-start(bf16[128,2048]{1,0:T(8,128)(2,1)S(1)} %multiply_convert_fusion.2), channel_id=1, source_target_pairs={{0,1},{1,0},{2,3},{3,2},{4,5},{5,4},{6,7},{7,6},{8,9},{9,8},{10,11... | collective-permute-start | bytes 1572872 | tf_op jit(solution)/shard_map/ppermute | solution.py:378
  78.1 28.1 %collective-permute-start.9 = (bf16[128,2048]{1,0:T(8,128)(2,1)S(1)}, bf16[128,2048]{1,0:T(8,128)(2,1)S(1)}, u32[]{:S(2)}, u32[]{:S(2)}) collective-permute-start(bf16[128,2048]{1,0:T(8,128)(2,1)S(1)} %multiply_convert_fusion.2), channel_id=1, source_target_pairs={{0,8},{8,0},{1,9},{9,1},{2,10},{10,2},{3,11},{11,3},{4,12},{12,4},... | collective-permute-start | bytes 1572872 | tf_op jit(solution)/shard_map/ppermute | solution.py:382
  80.4 25.8 %collective-permute-start.10 = (bf16[128,2048]{1,0:T(8,128)(2,1)S(1)}, bf16[128,2048]{1,0:T(8,128)(2,1)S(1)}, u32[]{:S(2)}, u32[]{:S(2)}) collective-permute-start(bf16[128,2048]{1,0:T(8,128)(2,1)S(1)} %multiply_convert_fusion.2), channel_id=1, source_target_pairs={{0,16},{16,0},{1,17},{17,1},{2,18},{18,2},{3,19},{19,3},{4,20},{20... | collective-permute-start | bytes 1572872 | tf_op jit(solution)/shard_map/ppermute | solution.py:374
  103.5 28.1 %collective-permute-start.19 = (bf16[4,256,640]{2,1,0:T(8,128)(2,1)S(1)}, bf16[4,256,640]{2,1,0:T(8,128)(2,1)S(1)}, u32[]{:S(2)}, u32[]{:S(2)}) collective-permute-start(bf16[4,256,640]{2,1,0:T(8,128)(2,1)S(1)} %collective-permute-done.18), channel_id=1, source_target_pairs={{0,2},{2,4},{4,6},{6,0},{1,3},{3,5},{5,7},{7,1},{8,10},{10,12},{12... | collective-permute-start | bytes 3932168 | tf_op jit(solution)/shard_map/ppermute | solution.py:395
  107.4 36.1 %collective-permute-start.12 = (bf16[64,2048]{1,0:T(8,128)(2,1)S(1)}, bf16[64,2048]{1,0:T(8,128)(2,1)}, u32[]{:S(2)}, u32[]{:S(2)}) collective-permute-start(bf16[64,2048]{1,0:T(8,128)(2,1)S(1)} %slice.714), channel_id=1, source_target_pairs={{0,8},{8,0},{1,9},{9,1},{2,10},{10,2},{3,11},{11,3},{4,12},{12,4},... | collective-permute-start | bytes 786440 | tf_op jit(solution)/shard_map/ppermute | solution.py:382
  113.6 41.0 %collective-permute-start.35 = (bf16[256,3072]{1,0:T(8,128)(2,1)}, bf16[256,3072]{1,0:T(8,128)(2,1)}, u32[]{:S(2)}, u32[]{:S(2)}) collective-permute-start(bf16[256,3072]{1,0:T(8,128)(2,1)} %get-tuple-element.365), channel_id=1, source_target_pairs={{0,8},{8,0},{1,9},{9,1},{2,10},{10,2},{3,11},{11,3},{4,12},{12,4},... | collective-permute-start | bytes 4718600 | tf_op jit(solution)/shard_map/ppermute | solution.py:382
  132.7 32.9 %collective-permute-start.36 = (bf16[256,3072]{1,0:T(8,128)(2,1)S(1)}, bf16[256,3072]{1,0:T(8,128)(2,1)}, u32[]{:S(2)}, u32[]{:S(2)}) collective-permute-start(bf16[256,3072]{1,0:T(8,128)(2,1)S(1)} %get-tuple-element.180.refs_0_.refs_8_), channel_id=1, source_target_pairs={{0,2},{2,4},{4,6},{6,0},{1,3},{3,5},{5,7},{7,1},{8,10},{10,12},{12... | collective-permute-start | bytes 4718600 | tf_op jit(solution)/shard_map/ppermute | solution.py:395
  165.6 32.7 %collective-permute-start.37 = (bf16[256,3072]{1,0:T(8,128)(2,1)}, bf16[256,3072]{1,0:T(8,128)(2,1)S(1)}, u32[]{:S(2)}, u32[]{:S(2)}) collective-permute-start(bf16[256,3072]{1,0:T(8,128)(2,1)} %collective-permute-done.35.refs_1_.refs_9_), channel_id=1, source_target_pairs={{0,2},{2,4},{4,6},{6,0},{1,3},{3,5},{5,7},{7,1},{8,10},{10,12},{12... | collective-permute-start | bytes 4718600 | tf_op jit(solution)/shard_map/ppermute | solution.py:395
  198.4 32.8 %collective-permute-start.38 = (bf16[256,3072]{1,0:T(8,128)(2,1)}, bf16[256,3072]{1,0:T(8,128)(2,1)S(1)}, u32[]{:S(2)}, u32[]{:S(2)}) collective-permute-start(bf16[256,3072]{1,0:T(8,128)(2,1)} %collective-permute-done.36.refs_2_.refs_10_), channel_id=1, source_target_pairs={{0,2},{2,4},{4,6},{6,0},{1,3},{3,5},{5,7},{7,1},{8,10},{10,12},{12... | collective-permute-start | bytes 4718600 | tf_op jit(solution)/shard_map/ppermute | solution.py:395
  231.2 32.8 %collective-permute-start.39 = (bf16[256,3072]{1,0:T(8,128)(2,1)S(1)}, bf16[256,3072]{1,0:T(8,128)(2,1)S(1)}, u32[]{:S(2)}, u32[]{:S(2)}) collective-permute-start(bf16[256,3072]{1,0:T(8,128)(2,1)S(1)} %collective-permute-done.37.refs_3_.refs_11_), channel_id=1, source_target_pairs={{0,2},{2,4},{4,6},{6,0},{1,3},{3,5},{5,7},{7,1},{8,10},{10,12},{12... | collective-permute-start | bytes 4718600 | tf_op jit(solution)/shard_map/ppermute | solution.py:395
  264.1 34.1 %collective-permute-start.40 = (bf16[256,3072]{1,0:T(8,128)(2,1)S(1)}, bf16[256,3072]{1,0:T(8,128)(2,1)S(1)}, u32[]{:S(2)}, u32[]{:S(2)}) collective-permute-start(bf16[256,3072]{1,0:T(8,128)(2,1)S(1)} %collective-permute-done.38.refs_4_.refs_12_), channel_id=1, source_target_pairs={{0,2},{2,4},{4,6},{6,0},{1,3},{3,5},{5,7},{7,1},{8,10},{10,12},{12... | collective-permute-start | bytes 4718600 | tf_op jit(solution)/shard_map/ppermute | solution.py:395
  275.2 26.6 %collective-permute-start.26 = (bf16[128,2048]{1,0:T(8,128)(2,1)S(1)}, bf16[128,2048]{1,0:T(8,128)(2,1)S(1)}, u32[]{:S(2)}, u32[]{:S(2)}) collective-permute-start(bf16[128,2048]{1,0:T(8,128)(2,1)S(1)} %multiply_convert_fusion.1), channel_id=1, source_target_pairs={{0,1},{1,0},{2,3},{3,2},{4,5},{5,4},{6,7},{7,6},{8,9},{9,8},{10,11... | collective-permute-start | bytes 1572872 | tf_op jit(solution)/shard_map/ppermute | solution.py:378
  298.1 33.1 %collective-permute-start.41 = (bf16[256,3072]{1,0:T(8,128)(2,1)S(1)}, bf16[256,3072]{1,0:T(8,128)(2,1)S(1)}, u32[]{:S(2)}, u32[]{:S(2)}) collective-permute-start(bf16[256,3072]{1,0:T(8,128)(2,1)S(1)} %collective-permute-done.39.refs_5_.refs_13_), channel_id=1, source_target_pairs={{0,2},{2,4},{4,6},{6,0},{1,3},{3,5},{5,7},{7,1},{8,10},{10,12},{12... | collective-permute-start | bytes 4718600 | tf_op jit(solution)/shard_map/ppermute | solution.py:395
  325.2 51.0 %collective-permute-start.50 = (bf16[256,3072]{1,0:T(8,128)(2,1)}, bf16[256,3072]{1,0:T(8,128)(2,1)S(1)}, u32[]{:S(2)}, u32[]{:S(2)}) collective-permute-start(bf16[256,3072]{1,0:T(8,128)(2,1)} %get-tuple-element.364), channel_id=1, source_target_pairs={{0,8},{8,0},{1,9},{9,1},{2,10},{10,2},{3,11},{11,3},{4,12},{12,4},... | collective-permute-start | bytes 4718600 | tf_op jit(solution)/shard_map/ppermute | solution.py:382
  326.4 28.1 %collective-permute-start.33 = (bf16[128,2048]{1,0:T(8,128)(2,1)S(1)}, bf16[128,2048]{1,0:T(8,128)(2,1)S(1)}, u32[]{:S(2)}, u32[]{:S(2)}) collective-permute-start(bf16[128,2048]{1,0:T(8,128)(2,1)S(1)} %pad_maximum_fusion.19), channel_id=1, source_target_pairs={{0,16},{16,0},{1,17},{17,1},{2,18},{18,2},{3,19},{19,3},{4,20},{20... | collective-permute-start | bytes 1572872 | tf_op jit(solution)/shard_map/ppermute | solution.py:374
  331.3 37.7 %collective-permute-start.42 = (bf16[128,2048]{1,0:T(8,128)(2,1)S(1)}, bf16[128,2048]{1,0:T(8,128)(2,1)S(1)}, u32[]{:S(2)}, u32[]{:S(2)}) collective-permute-start(bf16[128,2048]{1,0:T(8,128)(2,1)S(1)} %get-tuple-element.466), channel_id=1, source_target_pairs={{16,0},{18,8},{20,16},{22,24},{24,2},{26,10},{28,18},{30,26},{17,1... | collective-permute-start | bytes 1572872 | tf_op jit(solution)/shard_map/ppermute | solution.py:1061
  376.5 71.5 %collective-permute-start.51 = (bf16[2,256,3072]{2,1,0:T(8,128)(2,1)S(1)}, bf16[2,256,3072]{2,1,0:T(8,128)(2,1)S(1)}, u32[]{:S(2)}, u32[]{:S(2)}) collective-permute-start(bf16[2,256,3072]{2,1,0:T(8,128)(2,1)S(1)} %pad_maximum_fusion.1.refs_0_.refs_4_), channel_id=1, source_target_pairs={{0,2},{2,4},{4,6},{6,0},{1,3},{3,5},{5,7},{7,1},{8,10},{10,12},{12... | collective-permute-start | bytes 9437192 | tf_op jit(solution)/shard_map/ppermute | solution.py:395
  466.2 70.5 %collective-permute-start.62 = (bf16[2,256,3072]{2,1,0:T(8,128)(2,1)S(1)}, bf16[2,256,3072]{2,1,0:T(8,128)(2,1)S(1)}, u32[]{:S(2)}, u32[]{:S(2)}) collective-permute-start(bf16[2,256,3072]{2,1,0:T(8,128)(2,1)S(1)} %collective-permute-done.51.refs_1_.refs_5_), channel_id=1, source_target_pairs={{0,2},{2,4},{4,6},{6,0},{1,3},{3,5},{5,7},{7,1},{8,10},{10,12},{12... | collective-permute-start | bytes 9437192 | tf_op jit(solution)/shard_map/ppermute | solution.py:395
  489.2 49.4 %collective-permute-start.67 = (bf16[128,2048]{1,0:T(8,128)(2,1)S(1)}, bf16[128,2048]{1,0:T(8,128)(2,1)S(1)}, u32[]{:S(2)}, u32[]{:S(2)}) collective-permute-start(bf16[128,2048]{1,0:T(8,128)(2,1)S(1)} %broadcast_select_fusion.13), channel_id=1, source_target_pairs={{0,1},{1,0},{2,3},{3,2},{4,5},{5,4},{6,7},{7,6},{8,9},{9,8},{10,11... | collective-permute-start | bytes 1572872 | tf_op jit(solution)/shard_map/ppermute | solution.py:378
  489.4 49.2 %collective-permute-start.68 = (bf16[128,2048]{1,0:T(8,128)(2,1)S(1)}, bf16[128,2048]{1,0:T(8,128)(2,1)S(1)}, u32[]{:S(2)}, u32[]{:S(2)}) collective-permute-start(bf16[128,2048]{1,0:T(8,128)(2,1)S(1)} %broadcast_select_fusion.13), channel_id=1, source_target_pairs={{0,8},{8,0},{1,9},{9,1},{2,10},{10,2},{3,11},{11,3},{4,12},{12,4},... | collective-permute-start | bytes 1572872 | tf_op jit(solution)/shard_map/ppermute | solution.py:382
  491.3 47.3 %collective-permute-start.69 = (bf16[128,2048]{1,0:T(8,128)(2,1)S(1)}, bf16[128,2048]{1,0:T(8,128)(2,1)S(1)}, u32[]{:S(2)}, u32[]{:S(2)}) collective-permute-start(bf16[128,2048]{1,0:T(8,128)(2,1)S(1)} %broadcast_select_fusion.13), channel_id=1, source_target_pairs={{0,16},{16,0},{1,17},{17,1},{2,18},{18,2},{3,19},{19,3},{4,20},{20... | collective-permute-start | bytes 1572872 | tf_op jit(solution)/shard_map/ppermute | solution.py:374
  550.0 27.9 %collective-permute-start.74 = (bf16[128,2048]{1,0:T(8,128)(2,1)S(1)}, bf16[128,2048]{1,0:T(8,128)(2,1)S(1)}, u32[]{:S(2)}, u32[]{:S(2)}) collective-permute-start(bf16[128,2048]{1,0:T(8,128)(2,1)S(1)} %pad_maximum_fusion.25), channel_id=1, source_target_pairs={{0,16},{16,0},{1,17},{17,1},{2,18},{18,2},{3,19},{19,3},{4,20},{20... | collective-permute-start | bytes 1572872 | tf_op jit(solution)/shard_map/ppermute | solution.py:374
  555.8 71.4 %collective-permute-start.83 = (bf16[2,256,3072]{2,1,0:T(8,128)(2,1)S(1)}, bf16[2,256,3072]{2,1,0:T(8,128)(2,1)S(1)}, u32[]{:S(2)}, u32[]{:S(2)}) collective-permute-start(bf16[2,256,3072]{2,1,0:T(8,128)(2,1)S(1)} %collective-permute-done.62.refs_2_.refs_6_), channel_id=1, source_target_pairs={{0,2},{2,4},{4,6},{6,0},{1,3},{3,5},{5,7},{7,1},{8,10},{10,12},{12... | collective-permute-start | bytes 9437192 | tf_op jit(solution)/shard_map/ppermute | solution.py:395
  657.1 47.0 %collective-permute-start.86 = (bf16[2,256,2048]{2,1,0:T(8,128)(2,1)}, bf16[2,256,2048]{2,1,0:T(8,128)(2,1)}, u32[]{:S(2)}, u32[]{:S(2)}) collective-permute-start(bf16[2,256,2048]{2,1,0:T(8,128)(2,1)} %ffn_grad.16), channel_id=1, source_target_pairs={{2,0},{4,2},{6,4},{0,6},{3,1},{5,3},{7,5},{1,7},{10,8},{12,10},{14... | collective-permute-start | bytes 6291464 | tf_op jit(solution)/shard_map/ppermute | solution.py:400
  728.7 46.3 %collective-permute-start.100 = (bf16[2,256,2048]{2,1,0:T(8,128)(2,1)S(1)}, bf16[2,256,2048]{2,1,0:T(8,128)(2,1)S(1)}, u32[]{:S(2)}, u32[]{:S(2)}) collective-permute-start(bf16[2,256,2048]{2,1,0:T(8,128)(2,1)S(1)} %ffn_grad.18), channel_id=1, source_target_pairs={{2,0},{4,2},{6,4},{0,6},{3,1},{5,3},{7,5},{1,7},{10,8},{12,10},{14... | collective-permute-start | bytes 6291464 | tf_op jit(solution)/shard_map/ppermute | solution.py:400
  776.3 30.9 %collective-permute-start.101 = (bf16[2,256,1024]{2,1,0:T(8,128)(2,1)S(1)}, bf16[2,256,1024]{2,1,0:T(8,128)(2,1)S(1)}, u32[]{:S(2)}, u32[]{:S(2)}) collective-permute-start(bf16[2,256,1024]{2,1,0:T(8,128)(2,1)S(1)} %ffn_grad.19), channel_id=1, source_target_pairs={{2,0},{4,2},{6,4},{0,6},{3,1},{5,3},{7,5},{1,7},{10,8},{12,10},{14... | collective-permute-start | bytes 3145736 | tf_op jit(solution)/shard_map/ppermute | solution.py:400
  822.1 46.2 %collective-permute-start.108 = (bf16[2,256,2048]{2,1,0:T(8,128)(2,1)S(1)}, bf16[2,256,2048]{2,1,0:T(8,128)(2,1)S(1)}, u32[]{:S(2)}, u32[]{:S(2)}) collective-permute-start(bf16[2,256,2048]{2,1,0:T(8,128)(2,1)S(1)} %ffn_grad.20), channel_id=1, source_target_pairs={{2,0},{4,2},{6,4},{0,6},{3,1},{5,3},{7,5},{1,7},{10,8},{12,10},{14... | collective-permute-start | bytes 6291464 | tf_op jit(solution)/shard_map/ppermute | solution.py:400
  874.9 33.0 %collective-permute-start.117 = (bf16[2,256,1024]{2,1,0:T(8,128)(2,1)S(1)}, bf16[2,256,1024]{2,1,0:T(8,128)(2,1)S(1)}, u32[]{:S(2)}, u32[]{:S(2)}) collective-permute-start(bf16[2,256,1024]{2,1,0:T(8,128)(2,1)S(1)} %ffn_grad.21), channel_id=1, source_target_pairs={{2,0},{4,2},{6,4},{0,6},{3,1},{5,3},{7,5},{1,7},{10,8},{12,10},{14... | collective-permute-start | bytes 3145736 | tf_op jit(solution)/shard_map/ppermute | solution.py:400
  932.1 25.9 %collective-permute-start.120 = (bf16[256,2048]{1,0:T(8,128)(2,1)}, bf16[256,2048]{1,0:T(8,128)(2,1)}, u32[]{:S(2)}, u32[]{:S(2)}) collective-permute-start(bf16[256,2048]{1,0:T(8,128)(2,1)} %get-tuple-element.396), channel_id=1, source_target_pairs={{0,16},{16,0},{1,17},{17,1},{2,18},{18,2},{3,19},{19,3},{4,20},{20... | collective-permute-start | bytes 3145736 | tf_op jit(solution)/shard_map/ppermute | solution.py:374
  982.0 32.1 %collective-permute-start.151 = (bf16[64,2048]{1,0:T(8,128)(2,1)S(1)}, bf16[64,2048]{1,0:T(8,128)(2,1)}, u32[]{:S(2)}, u32[]{:S(2)}) collective-permute-start(bf16[64,2048]{1,0:T(8,128)(2,1)S(1)} %get-tuple-element.446), channel_id=1, source_target_pairs={{0,1},{1,0},{2,3},{3,2},{4,5},{5,4},{6,7},{7,6},{8,9},{9,8},{10,11... | collective-permute-start | bytes 786440 | tf_op jit(solution)/shard_map/ppermute | solution.py:378
  996.4 52.5 %collective-permute-start.137 = (bf16[2,256,2048]{2,1,0:T(8,128)(2,1)}, bf16[2,256,2048]{2,1,0:T(8,128)(2,1)}, u32[]{:S(2)}, u32[]{:S(2)}) collective-permute-start(bf16[2,256,2048]{2,1,0:T(8,128)(2,1)} %ffn_grad.24), channel_id=1, source_target_pairs={{2,0},{4,2},{6,4},{0,6},{3,1},{5,3},{7,5},{1,7},{10,8},{12,10},{14... | collective-permute-start | bytes 6291464 | tf_op jit(solution)/shard_map/ppermute | solution.py:400
  1007.7 29.8 %collective-permute-start.129 = (bf16[128,2048]{1,0:T(8,128)(2,1)}, bf16[128,2048]{1,0:T(8,128)(2,1)}, u32[]{:S(2)}, u32[]{:S(2)}) collective-permute-start(bf16[128,2048]{1,0:T(8,128)(2,1)} %convert_element_type.336), channel_id=1, source_target_pairs={{0,1},{1,0},{2,3},{3,2},{4,5},{5,4},{6,7},{7,6},{8,9},{9,8},{10,11... | collective-permute-start | bytes 1572872 | tf_op jit(solution)/shard_map/ppermute | solution.py:378
  1008.0 29.5 %collective-permute-start.130 = (bf16[128,2048]{1,0:T(8,128)(2,1)}, bf16[128,2048]{1,0:T(8,128)(2,1)}, u32[]{:S(2)}, u32[]{:S(2)}) collective-permute-start(bf16[128,2048]{1,0:T(8,128)(2,1)} %convert_element_type.336), channel_id=1, source_target_pairs={{0,8},{8,0},{1,9},{9,1},{2,10},{10,2},{3,11},{11,3},{4,12},{12,4},... | collective-permute-start | bytes 1572872 | tf_op jit(solution)/shard_map/ppermute | solution.py:382
  1009.2 28.3 %collective-permute-start.131 = (bf16[128,2048]{1,0:T(8,128)(2,1)}, bf16[128,2048]{1,0:T(8,128)(2,1)}, u32[]{:S(2)}, u32[]{:S(2)}) collective-permute-start(bf16[128,2048]{1,0:T(8,128)(2,1)} %convert_element_type.336), channel_id=1, source_target_pairs={{0,16},{16,0},{1,17},{17,1},{2,18},{18,2},{3,19},{19,3},{4,20},{20... | collective-permute-start | bytes 1572872 | tf_op jit(solution)/shard_map/ppermute | solution.py:374
  1078.7 27.0 %collective-permute-start.141 = (bf16[256,2048]{1,0:T(8,128)(2,1)S(1)}, bf16[256,2048]{1,0:T(8,128)(2,1)S(1)}, u32[]{:S(2)}, u32[]{:S(2)}) collective-permute-start(bf16[256,2048]{1,0:T(8,128)(2,1)S(1)} %get-tuple-element.394), channel_id=1, source_target_pairs={{0,16},{16,0},{1,17},{17,1},{2,18},{18,2},{3,19},{19,3},{4,20},{20... | collective-permute-start | bytes 3145736 | tf_op jit(solution)/shard_map/ppermute | solution.py:374
  1087.7 51.6 %collective-permute-start.154 = (bf16[128,2048]{1,0:T(8,128)(2,1)}, bf16[128,2048]{1,0:T(8,128)(2,1)}, u32[]{:S(2)}, u32[]{:S(2)}) collective-permute-start(bf16[128,2048]{1,0:T(8,128)(2,1)} %pad_maximum_fusion.39), channel_id=1, source_target_pairs={{0,8},{8,0},{1,9},{9,1},{2,10},{10,2},{3,11},{11,3},{4,12},{12,4},... | collective-permute-start | bytes 1572872 | tf_op jit(solution)/shard_map/ppermute | solution.py:382
  1111.9 27.3 %collective-permute-start.153 = (bf16[128,2048]{1,0:T(8,128)(2,1)}, bf16[128,2048]{1,0:T(8,128)(2,1)}, u32[]{:S(2)}, u32[]{:S(2)}) collective-permute-start(bf16[128,2048]{1,0:T(8,128)(2,1)} %pad_maximum_fusion.38), channel_id=1, source_target_pairs={{0,1},{1,0},{2,3},{3,2},{4,5},{5,4},{6,7},{7,6},{8,9},{9,8},{10,11... | collective-permute-start | bytes 1572872 | tf_op jit(solution)/shard_map/ppermute | solution.py:378
  1134.9 45.7 %collective-permute-start.158 = (bf16[2,256,2048]{2,1,0:T(8,128)(2,1)S(1)}, bf16[2,256,2048]{2,1,0:T(8,128)(2,1)S(1)}, u32[]{:S(2)}, u32[]{:S(2)}) collective-permute-start(bf16[2,256,2048]{2,1,0:T(8,128)(2,1)S(1)} %ffn_grad.26), channel_id=1, source_target_pairs={{2,0},{4,2},{6,4},{0,6},{3,1},{5,3},{7,5},{1,7},{10,8},{12,10},{14... | collective-permute-start | bytes 6291464 | tf_op jit(solution)/shard_map/ppermute | solution.py:400
  1151.4 33.1 %collective-permute-start.169 = (bf16[256,640]{1,0:T(8,128)(2,1)S(1)}, bf16[256,640]{1,0:T(8,128)(2,1)S(1)}, u32[]{:S(2)}, u32[]{:S(2)}) collective-permute-start(bf16[256,640]{1,0:T(8,128)(2,1)S(1)} %get-tuple-element.481), channel_id=1, source_target_pairs={{0,8},{8,0},{1,9},{9,1},{2,10},{10,2},{3,11},{11,3},{4,12},{12,4},... | collective-permute-start | bytes 983048 | tf_op jit(solution)/shard_map/ppermute | solution.py:382
  1152.7 36.9 %collective-permute-start.156 = (f32[2,1024]{1,0:T(2,128)S(1)}, f32[2,1024]{1,0:T(2,128)S(1)}, u32[]{:S(2)}, u32[]{:S(2)}) collective-permute-start(f32[2,1024]{1,0:T(2,128)S(1)} %broadcast_select_fusion.24), channel_id=1, source_target_pairs={{0,8},{8,0},{1,9},{9,1},{2,10},{10,2},{3,11},{11,3},{4,12},{12,4},... | collective-permute-start | bytes 24584 | tf_op jit(solution)/shard_map/ppermute | solution.py:382
  1202.4 44.1 %collective-permute-start.160 = (bf16[2,256,2048]{2,1,0:T(8,128)(2,1)S(1)}, bf16[2,256,2048]{2,1,0:T(8,128)(2,1)S(1)}, u32[]{:S(2)}, u32[]{:S(2)}) collective-permute-start(bf16[2,256,2048]{2,1,0:T(8,128)(2,1)S(1)} %ffn_grad.29), channel_id=1, source_target_pairs={{2,0},{4,2},{6,4},{0,6},{3,1},{5,3},{7,5},{1,7},{10,8},{12,10},{14... | collective-permute-start | bytes 6291464 | tf_op jit(solution)/shard_map/ppermute | solution.py:400
  1272.9 29.5 %collective-permute-start.173 = (bf16[256,1024]{1,0:T(8,128)(2,1)S(1)}, bf16[256,1024]{1,0:T(8,128)(2,1)S(1)}, u32[]{:S(2)}, u32[]{:S(2)}) collective-permute-start(bf16[256,1024]{1,0:T(8,128)(2,1)S(1)} %get-tuple-element.435), channel_id=1, source_target_pairs={{0,8},{8,0},{1,9},{9,1},{2,10},{10,2},{3,11},{11,3},{4,12},{12,4},... | collective-permute-start | bytes 1572872 | tf_op jit(solution)/shard_map/ppermute | solution.py:382
  1278.9 79.6 %collective-permute-start.172 = (bf16[2,256,2048]{2,1,0:T(8,128)(2,1)}, bf16[2,256,2048]{2,1,0:T(8,128)(2,1)S(1)}, u32[]{:S(2)}, u32[]{:S(2)}) collective-permute-start(bf16[2,256,2048]{2,1,0:T(8,128)(2,1)} %pad_maximum_fusion.9), channel_id=1, source_target_pairs={{0,16},{16,0},{1,17},{17,1},{2,18},{18,2},{3,19},{19,3},{4,20},{20... | collective-permute-start | bytes 6291464 | tf_op jit(solution)/shard_map/ppermute | solution.py:374
  1302.4 30.2 %collective-permute-start.165 = (bf16[128,2048]{1,0:T(8,128)(2,1)S(1)}, bf16[128,2048]{1,0:T(8,128)(2,1)S(1)}, u32[]{:S(2)}, u32[]{:S(2)}) collective-permute-start(bf16[128,2048]{1,0:T(8,128)(2,1)S(1)} %copy-done.206), channel_id=1, source_target_pairs={{0,16},{8,18},{16,20},{24,22},{2,24},{10,26},{18,28},{26,30},{1,17... | collective-permute-start | bytes 1572872 | tf_op jit(solution)/shard_map/ppermute | solution.py:1111
  1304.5 30.4 %collective-permute-start.174 = (bf16[2,256,1024]{2,1,0:T(8,128)(2,1)S(1)}, bf16[2,256,1024]{2,1,0:T(8,128)(2,1)S(1)}, u32[]{:S(2)}, u32[]{:S(2)}) collective-permute-start(bf16[2,256,1024]{2,1,0:T(8,128)(2,1)S(1)} %pad_maximum_fusion.12), channel_id=1, source_target_pairs={{0,16},{16,0},{1,17},{17,1},{2,18},{18,2},{3,19},{19,3},{4,20},{20... | collective-permute-start | bytes 3145736 | tf_op jit(solution)/shard_map/ppermute | solution.py:374
  (348 other events, 7030.2 us)
